TPU v7x, 128 devices: a whole 4x4x4 slice. The times are simulated.
128 devices in a mesh: row: 8 (over y, core), col: 16 (over z, x).
Axes of the slice: x: 4, y: 4, z: 4, core: 2. Of those that a mesh axis runs over, the one named last changes fastest.
Arguments:
- blocks: bfloat16 [512, 10, 256, 256], P(('row', 'col')), may hold values from -0.0625 to 0.0625
- block_scales: float32 [512, 10], P(('row', 'col')), may hold values from 0.15 to 0.6
- columns: int32 [512, 10], P(('row', 'col')), may hold values from 0 to 511, as said below
- live: int32 [512], P(('row', 'col')), may hold values from 3 to 10
- onsite: float32 [131072], P(('row', 'col')), may hold values from -1 to 1
- start_vectors: bfloat16 [131072, 128], P(('row', 'col')), may hold values from -6 to 6
Outputs:
- basis: float32 [131072, 128], P(('row', 'col'))
Inputs may be any that keep to these rules, and one draw needn't show every extreme that they name: `columns`: slot 0 of each block row is the row itself; every column lies within 4 block rows of its row, cyclically over 512, and that distance is reached in both directions in every draw.
All inputs are finite; a program needn't handle non-finite values.
Results may differ from a plain program's by a relative error of at most 0.014.
Values may be sent and summed in bfloat16 or wider, within the bound.
No kernel may reach another device: no remote copies, remote signals or barrier semaphores. Data moves between devices by JAX's collectives and lax.ppermute only.
A program may use at most 128 MiB of HBM per device.

v0:
```python
import functools

import jax
import jax.numpy as jnp
import numpy as np
from jax import lax
from jax.experimental import pallas as pl
from jax.experimental.pallas import tpu as pltpu
from jax.sharding import PartitionSpec as P

DEG = 5
B = 256
K = 128
ROWS = 4
OWN = ROWS * B
REACH = 4
SPAN = 2 * REACH + 1
AXES = ("row", "col")
ALPHA = 2.0 / 1.1
SHIFT = 0.2
F32 = jnp.float32
BF16 = jnp.bfloat16
EDGE = (8, 9, 2, 3)
TO_RIGHT = ((2, 10), (3, 10), (3, 11))
TO_LEFT = ((0, 0), (0, 1), (1, 1))
HANDED = 3 * 2 * B
T = 8


def rows(i, n=1):
    return pl.ds(i * B, n * B)


def dot(a, b):
    return jnp.dot(a, b, preferred_element_type=F32)


def read_block(ref, i):
    return jnp.concatenate([ref[rows(2 * i), :], ref[rows(2 * i + 1), :]], axis=1)


def flip(block):
    return block.astype(F32).T


def prep_kernel(total, scales, columns, live, blocks, y0, own, edge, to_e, to_o, buf, acc, head, after, sem):
    copies = [pltpu.make_async_copy(blocks.at[a], buf.at[a], sem.at[a]) for a in range(ROWS)]
    for copy in copies:
        copy.start()
    first = lax.axis_index(AXES) * ROWS
    for a in range(ROWS):
        for o in range(SPAN):
            head[a, o] = -1

        def chain(s, carry, a=a):
            o = lax.rem(columns[a, s] - (first + a) + REACH + total, total)
            after[a, s] = head[a, o]
            head[a, o] = s
            return carry

        lax.fori_loop(0, live[a], chain, 0)
    turned = flip(y0[...]).astype(BF16)
    for target in (to_e, to_o):
        target[pl.ds(HANDED + 2 * B, OWN), :] = y0[...]
    even = lax.rem(lax.axis_index(AXES), 2) == 0

    def put_message(right, start, value):
        for case, target in ((even, to_e if right else to_o), (~even, to_o if right else to_e)):

            @pl.when(case)
            def _(target=target):
                target[pl.ds(start, value.shape[0]), :] = value

    def put(a, p, value):
        if 4 <= p < 8:
            own[rows(a), rows(p - 4)] = value
        elif p in EDGE:
            edge[rows(a), rows(EDGE.index(p))] = value
        else:
            right = p > 8
            i = (TO_RIGHT if right else TO_LEFT).index((a, p))
            put_message(right, 2 * i * B, value[:, :K])
            put_message(right, (2 * i + 1) * B, value[:, K:])

    def scaled(a, s):
        return (scales[a, s] * ALPHA) * buf[a, s].astype(F32)

    def place(a, o):
        s = head[a, o]

        @pl.when(s < 0)
        def _():
            put(a, a + o, jnp.zeros((B, B), BF16))

        @pl.when(s >= 0)
        def _():
            rest = after[a, jnp.maximum(s, 0)]

            @pl.when(rest < 0)
            def _():
                put(a, a + o, scaled(a, s).astype(BF16))

            @pl.when(rest >= 0)
            def _():
                acc[...] = scaled(a, s)

                def more(t):
                    acc[...] = acc[...] + scaled(a, t)
                    return after[a, t]

                lax.while_loop(lambda t: t >= 0, more, rest)
                put(a, a + o, acc[...].astype(BF16))

    edge[rows(0), rows(1)] = jnp.zeros((B, B), BF16)
    edge[rows(3), rows(2)] = jnp.zeros((B, B), BF16)
    for a in range(ROWS):
        copies[a].wait()
        for o in range(SPAN):
            place(a, o)
    terms = dot(turned, edge[...]).T.astype(BF16)
    put_message(True, HANDED, terms[: 2 * B])
    put_message(False, HANDED, terms[2 * B :])


def first_local_kernel(own, edge, onsite, y0, diag, sym, edge_t, base):
    for a in range(ROWS):
        for b in range(a + 1):
            value = own[rows(a), rows(b)].astype(F32) + flip(own[rows(b), rows(a)])
            sym[rows(a), rows(b)] = value.astype(BF16)
            if b < a:
                sym[rows(b), rows(a)] = value.T.astype(BF16)
    for a in range(ROWS):
        for j in range(4):
            edge_t[rows(j), rows(a)] = flip(edge[rows(a), rows(j)]).astype(BF16)
    diag[...] = ALPHA * (onsite[...] - SHIFT)
    base[...] = diag[...] * y0[...].astype(F32) + dot(sym[...], y0[...])


def by_parity(body):
    parity = lax.rem(lax.axis_index(AXES), 2)
    for value in (0, 1):

        @pl.when(parity == value)
        def _(even=value == 0):
            body(even)


def from_right(a, edge, got, halo=0, terms=2 * B):
    wide = 1 if a == 0 else 2
    total = dot(edge[rows(a), rows(0, wide)], got[pl.ds(halo, wide * B), :])
    if a >= 2:
        total += got[pl.ds(terms + (a - 2) * B, B), :].astype(F32)
    return total


def from_left(a, edge, got, halo=0, terms=2 * B):
    skip = 1 if a == ROWS - 1 else 0
    total = dot(edge[rows(a), rows(2 + skip, 2 - skip)], got[pl.ds(halo + skip * B, (2 - skip) * B), :])
    if a < 2:
        total += got[pl.ds(terms + a * B, B), :].astype(F32)
    return total


def send_parts(edge_t, y, send_right, send_left):
    send_right[pl.ds(0, 2 * B), :] = y[pl.ds(2 * B, 2 * B), :]
    send_left[pl.ds(0, 2 * B), :] = y[pl.ds(0, 2 * B), :]
    send_right[pl.ds(2 * B, B), :] = dot(edge_t[rows(0), :], y[...]).astype(BF16)
    send_right[pl.ds(3 * B, B), :] = dot(edge_t[rows(1), rows(1, 3)], y[rows(1, 3), :]).astype(BF16)
    send_left[pl.ds(2 * B, B), :] = dot(edge_t[rows(2), rows(0, 3)], y[rows(0, 3), :]).astype(BF16)
    send_left[pl.ds(3 * B, B), :] = dot(edge_t[rows(3), :], y[...]).astype(BF16)


def first_post_kernel(base, edge_in, edge_t_in, to_e, to_o, got_e, got_o, edge, edge_t, y, send_e, send_o):
    edge[...] = edge_in[...]
    edge_t[...] = edge_t_in[...]

    def body(even):
        to_right, to_left = (to_e, to_o) if even else (to_o, to_e)
        got_right, got_left = (got_e, got_o) if even else (got_o, got_e)
        for i, (r, c) in enumerate(TO_LEFT):
            block = read_block(got_right, i).astype(F32)
            edge_t[rows(r), rows(c)] = (edge_t[rows(r), rows(c)].astype(F32) + block).astype(BF16)
            edge[rows(c), rows(r)] = (edge[rows(c), rows(r)].astype(F32) + block.T).astype(BF16)
        for i, (c, p) in enumerate(TO_RIGHT):
            block = read_block(got_left, i).astype(F32)
            r = p - 8
            edge_t[rows(c), rows(r)] = (edge_t[rows(c), rows(r)].astype(F32) + block).astype(BF16)
            edge[rows(r), rows(c)] = (edge[rows(r), rows(c)].astype(F32) + block.T).astype(BF16)
        halo = HANDED + 2 * B
        for a in range(ROWS):
            total = base[rows(a), :] + from_right(a, edge, got_right, halo, HANDED)
            total += from_left(a, edge, got_left, halo + 2 * B, HANDED)
            for places, source, got, start in ((TO_LEFT, to_left, got_left, 0), (TO_RIGHT, to_right, got_right, 8)):
                for i, (row, p) in enumerate(places):
                    if row == a:
                        total += dot(read_block(source, i), got[pl.ds(halo + (p - start) * B, B), :])
            y[rows(a), :] = (0.5 * total).astype(BF16)
        send_parts(edge_t, y, *((send_e, send_o) if even else (send_o, send_e)))

    by_parity(body)


def local_kernel(sym, diag, y, older, edge, got_e, base):
    base[...] = diag[...] * y[...].astype(F32) - older[...].astype(F32) + dot(sym[...], y[...])

    def body(even):
        for a in range(ROWS):
            base[rows(a), :] += (from_right if even else from_left)(a, edge, got_e)

    by_parity(body)


def receive(even, base, edge, got_o, y):
    for a in range(ROWS):
        y[rows(a), :] = (base[rows(a), :] + (from_left if even else from_right)(a, edge, got_o)).astype(BF16)


def post_kernel(base, edge, edge_t, got_o, y, send_e, send_o):
    def body(even):
        receive(even, base, edge, got_o, y)
        send_parts(edge_t, y, *((send_e, send_o) if even else (send_o, send_e)))

    by_parity(body)


def last_kernel(base, edge, got_o, y, gram):
    by_parity(lambda even: receive(even, base, edge, got_o, y))
    gram[...] = lax.dot_general(y[...], y[...], (((0,), (0,)), ((), ())), preferred_element_type=F32)


def lane_fill(x, c):
    return jnp.take_along_axis(x, jnp.full((T, K), c, jnp.int32), axis=1)


def row_fill(x, j):
    return jnp.take_along_axis(x, jnp.full((T, K), j, jnp.int32), axis=0)


def inverse_factor(gram, inverse):
    count = K // T
    lane = lax.broadcasted_iota(jnp.int32, (T, K), 1)
    sub = lax.broadcasted_iota(jnp.int32, (T, K), 0)
    tiles = [gram[pl.ds(T * t, T), :] for t in range(count)]
    for k in range(count):
        first = T * k
        inside = (lane >= first) & (lane < first + T)
        spread = [lane_fill(tiles[k], first + c) for c in range(T)]
        rest = jnp.where(inside, 0.0, tiles[k])
        steps = []
        scale = jnp.zeros((T, K), F32)
        for j in range(T):
            pivot = row_fill(spread[j], j)
            inv = 1.0 / pivot
            ratios = {c: row_fill(spread[c], j) * inv for c in range(j + 1, T)}
            row = jnp.where(lane == first + j, 1.0, row_fill(rest, j)) * inv
            steps.append((ratios, row))
            rest = rest - jnp.where(sub > j, spread[j], 0.0) * row
            for c in range(j + 1, T):
                spread[c] = spread[c] - spread[j] * ratios[c]
            scale = jnp.where(sub == j, lax.rsqrt(pivot), scale)
        unit = jnp.where(lane < first + sub, rest, jnp.where(lane == first + sub, 1.0, 0.0))
        inverse[pl.ds(first, T), :] = unit * scale
        for t in range(k + 1, count):
            factors = [lane_fill(tiles[t], first + c) for c in range(T)]
            value = jnp.where(inside, 0.0, tiles[t])
            for j, (ratios, row) in enumerate(steps):
                value = value - factors[j] * row
                for c in range(j + 1, T):
                    factors[c] = factors[c] - factors[j] * ratios[c]
            tiles[t] = value


def finish_kernel(scale, gram, y, basis, inverse):
    inverse_factor(gram, inverse)
    value = inverse[...] * scale
    high = value.astype(BF16)
    low = (value - high.astype(F32)).astype(BF16)
    dims = (((1,), (1,)), ((), ()))
    basis[...] = lax.dot_general(y[...], high, dims, preferred_element_type=F32) + lax.dot_general(
        y[...], low, dims, preferred_element_type=F32
    )


VMEM = pl.BlockSpec(memory_space=pltpu.VMEM)
SMEM = pl.BlockSpec(memory_space=pltpu.SMEM)
HBM = pl.BlockSpec(memory_space=pltpu.HBM)
LIMIT = 20 * 1024 * 1024
PREP_LIMIT = 57 * 1000 * 1000


def call(kernel, outs, specs, flops, size, scratch=(), aliases=None, limit=LIMIT):
    return pl.pallas_call(
        kernel,
        out_shape=[jax.ShapeDtypeStruct(*out) for out in outs],
        in_specs=list(specs),
        out_specs=[VMEM] * len(outs),
        scratch_shapes=list(scratch),
        input_output_aliases=aliases or {},
        cost_estimate=pl.CostEstimate(flops=flops, bytes_accessed=size, transcendentals=0),
        compiler_params=pltpu.CompilerParams(vmem_limit_bytes=limit),
    )


def swap_o(value):
    count = lax.axis_size(AXES)
    return lax.ppermute(value, AXES, [(i, (i + 1 if i % 2 else i - 1) % count) for i in range(count)])


def swap_e(value):
    return lax.ppermute(value, AXES, [(i, i ^ 1) for i in range(lax.axis_size(AXES))])


def group_sum(value, stride, size):
    count = lax.axis_size(AXES)
    parts = [value]
    for step in range(1, size):
        pairs = []
        for i in range(count):
            digit = (i // stride) % size
            partner = digit ^ step if size & (size - 1) == 0 else (digit + step) % size
            pairs.append((i, i + (partner - digit) * stride))
        parts.append(lax.ppermute(value, AXES, pairs))
    return sum(parts[1:], parts[0])


def digits():
    out, stride = [], 1
    for axis, cut in (("col", 4), ("row", 2)):
        left = lax.axis_size(axis)
        while left > 1:
            size = cut if left % cut == 0 else left
            out.append((stride, size))
            stride *= size
            left //= size
            cut = left if axis == "row" else cut
    return out


def local(blocks, block_scales, columns, live, onsite, start_vectors):
    slots = columns.shape[1]
    total = ROWS * lax.axis_size(AXES)
    column = ((OWN, 1), F32)
    tall = ((OWN, K), BF16)
    tall32 = ((OWN, K), F32)
    square = ((OWN, OWN), BF16)
    message = ((HANDED + 2 * B + OWN, K), BF16)
    product = 2 * OWN * OWN * K

    y0 = start_vectors
    own, edge, to_e, to_o = call(
        functools.partial(prep_kernel, total),
        [square, square, message, message],
        [SMEM, SMEM, SMEM, HBM, VMEM],
        product,
        10_000_000,
        [
            pltpu.VMEM((ROWS, slots, B, B), BF16),
            pltpu.VMEM((B, B), F32),
            pltpu.SMEM((ROWS, SPAN), jnp.int32),
            pltpu.SMEM((ROWS, slots), jnp.int32),
            pltpu.SemaphoreType.DMA((ROWS,)),
        ],
        limit=PREP_LIMIT,
    )(block_scales, columns, live, blocks, y0)
    got_o, got_e = swap_o(to_o), swap_e(to_e)
    diag, sym, edge_t, base = call(first_local_kernel, [column, square, square, tall32], [VMEM] * 4, product, 10_000_000)(
        own, edge, onsite[:, None], y0
    )
    edge, edge_t, y, send_e, send_o = call(
        first_post_kernel, [square, square, tall, tall, tall], [VMEM] * 7, 2 * product, 9_000_000, (), {1: 0, 2: 1}
    )(base, edge, edge_t, to_e, to_o, got_e, got_o)
    older = y0
    for step in range(1, DEG):
        got_o, got_e = swap_o(send_o), swap_e(send_e)
        base = call(local_kernel, [tall32], [VMEM] * 6, product, 3_500_000)(sym, diag, y, older, edge, got_e)[0]
        older = y
        if step < DEG - 1:
            y, send_e, send_o = call(post_kernel, [tall, tall, tall], [VMEM] * 4, 2 * product, 6_000_000)(
                base, edge, edge_t, got_o
            )
        else:
            y, gram = call(last_kernel, [tall, ((K, K), F32)], [VMEM] * 3, product, 4_000_000)(base, edge, got_o)
    for stride, size in digits():
        gram = group_sum(gram, stride, size)
    scale = float(np.sqrt(total * B))
    return call(
        functools.partial(finish_kernel, scale), [tall32], [VMEM] * 2, 2 * product, 1_000_000, [pltpu.VMEM((K, K), F32)]
    )(gram, y)[0]


def solution(mesh):
    return jax.shard_map(
        local,
        mesh=mesh,
        in_specs=(
            P(AXES, None, None, None),
            P(AXES, None),
            P(AXES, None),
            P(AXES),
            P(AXES),
            P(AXES, None),
        ),
        out_specs=P(AXES, None),
        check_vma=False,
    )
```

profile of v0, /device:TPU:0, one launch (start us, length us, event | category | flops | bytes accessed | tf_op | source)
XLA Modules:
  0.0 123.4 jit_solution(984783114212410932)
XLA Ops:
  0.0 0.0 copy-start.2
  0.0 0.0 copy-start.6
  0.0 7.2 %shard_map.64 = (bf16[1024,1024]{1,0:T(8,128)(2,1)}, bf16[1024,1024]{1,0:T(8,128)(2,1)}, bf16[3072,128]{1,0:T(8,128)(2,1)}, bf16[3072,128]{1,0:T(8,128)(2,1)}) custom-call(f32[4,10]{1,0:T(4,128)} %scales.1, s32[4,10]{1,0:T(4,128)} %columns.1, s32[4]{0:T(128)} %live.1, bf16[4,10,256,256]{3,2,1,0:T(8,128)(2,1)} %blocks.1, bf16[1024,128]{1,0:T(8,128)(2,1)} %older.1), custom_call_target="tpu_custom_call" | custom-call | flops 268435456 | bytes 10000000 | tf_op jit(solution)/shard_map/pallas_call | solution.py:350
  7.2 1.3 %collective-permute-start = (bf16[3072,128]{1,0:T(8,128)(2,1)}, bf16[3072,128]{1,0:T(8,128)(2,1)S(1)}, u32[]{:S(2)}, u32[]{:S(2)}) collective-permute-start(bf16[3072,128]{1,0:T(8,128)(2,1)} %get-tuple-element.35.to_e), channel_id=1, source_target_pairs={{0,1},{1,0},{2,3},{3,2},{4,5},{5,4},{6,7},{7,6},{8,9},{9,8},{10,11... | collective-permute-start | bytes 2359304 | tf_op jit(solution)/shard_map/ppermute | solution.py:310
  8.5 7.5 %collective-permute-start.1 = (bf16[3072,128]{1,0:T(8,128)(2,1)}, bf16[3072,128]{1,0:T(8,128)(2,1)S(1)}, u32[]{:S(2)}, u32[]{:S(2)}) collective-permute-start(bf16[3072,128]{1,0:T(8,128)(2,1)} %get-tuple-element.36.to_o), channel_id=1, source_target_pairs={{0,127},{1,2},{2,1},{3,4},{4,3},{5,6},{6,5},{7,8},{8,7},{9,10},{10... | collective-permute-start | bytes 2359304 | tf_op jit(solution)/shard_map/ppermute | solution.py:306
  16.0 0.0 copy-done.6
  16.0 0.2 copy.9.onsite
  16.2 0.0 copy-done.2
  16.2 0.0 copy-start
  16.3 1.6 %copy-done = bf16[1024,1024]{1,0:T(8,128)(2,1)S(1)} copy-done((bf16[1024,1024]{1,0:T(8,128)(2,1)S(1)}, bf16[1024,1024]{1,0:T(8,128)(2,1)}, u32[]{:S(2)}) %copy-start) | copy-done | bytes 2097176
  17.8 0.0 copy-start.3
  17.8 1.6 %copy-done.3 = bf16[1024,1024]{1,0:T(8,128)(2,1)S(1)} copy-done((bf16[1024,1024]{1,0:T(8,128)(2,1)S(1)}, bf16[1024,1024]{1,0:T(8,128)(2,1)}, u32[]{:S(2)}) %copy-start.3) | copy-done | bytes 2097176
  19.4 1.6 %shard_map.65 = (f32[1024,1]{1,0:T(8,128)S(1)}, bf16[1024,1024]{1,0:T(8,128)(2,1)S(1)}, bf16[1024,1024]{1,0:T(8,128)(2,1)S(1)}, f32[1024,128]{1,0:T(8,128)S(1)}) custom-call(bf16[1024,1024]{1,0:T(8,128)(2,1)S(1)} %copy-done.3, bf16[1024,1024]{1,0:T(8,128)(2,1)S(1)} %copy-done, f32[1024,1]{1,0:T(8,128)S(1)} %copy.9.onsite, bf16[1024,128]{1,0:T(8,128)(2,1)S(1)} %copy-done.2), custom_call_target="tpu_custom_call" | custom-call | flops 268435456 | bytes 10000000 | tf_op jit(solution)/shard_map/pallas_call | solution.py:366
  21.1 5.4 %collective-permute-done.got_e = bf16[3072,128]{1,0:T(8,128)(2,1)S(1)} collective-permute-done((bf16[3072,128]{1,0:T(8,128)(2,1)}, bf16[3072,128]{1,0:T(8,128)(2,1)S(1)}, u32[]{:S(2)}, u32[]{:S(2)}) %collective-permute-start) | collective-permute-done | bytes 786464 | tf_op jit(solution)/shard_map/ppermute | solution.py:310
  26.5 7.2 %collective-permute-done.1.got_o = bf16[3072,128]{1,0:T(8,128)(2,1)S(1)} collective-permute-done((bf16[3072,128]{1,0:T(8,128)(2,1)}, bf16[3072,128]{1,0:T(8,128)(2,1)S(1)}, u32[]{:S(2)}, u32[]{:S(2)}) %collective-permute-start.1) | collective-permute-done | bytes 786464 | tf_op jit(solution)/shard_map/ppermute | solution.py:306
  33.6 0.0 copy-done.1
  33.6 0.0 copy-done.4
  33.6 0.0 copy-done.5
  33.7 2.1 %shard_map.66 = (bf16[1024,1024]{1,0:T(8,128)(2,1)S(1)}, bf16[1024,1024]{1,0:T(8,128)(2,1)S(1)}, bf16[1024,128]{1,0:T(8,128)(2,1)S(1)}, bf16[1024,128]{1,0:T(8,128)(2,1)S(1)}, bf16[1024,128]{1,0:T(8,128)(2,1)S(1)}) custom-call(f32[1024,128]{1,0:T(8,128)S(1)} %get-tuple-element.33.base, ...), custom_call_target="tpu_custom_call", output_to_operand_aliasing={{0}: (1, {}), {1}: (2, {})} | custom-call | flops 536870912 | bytes 9000000 | tf_op jit(solution)/shard_map/pallas_call | solution.py:369
  35.8 0.1 collective-permute-start.2
  35.9 7.0 %collective-permute-start.3 = (bf16[1024,128]{1,0:T(8,128)(2,1)S(1)}, bf16[1024,128]{1,0:T(8,128)(2,1)S(1)}, u32[]{:S(2)}, u32[]{:S(2)}) collective-permute-start(bf16[1024,128]{1,0:T(8,128)(2,1)S(1)} %get-tuple-element.41), channel_id=1, source_target_pairs={{0,127},{1,2},{2,1},{3,4},{4,3},{5,6},{6,5},{7,8},{8,7},{9,10},{10... | collective-permute-start | bytes 786440 | tf_op jit(solution)/shard_map/ppermute | solution.py:306
  42.9 0.8 collective-permute-done.2.got_e
  43.7 1.1 shard_map.67.base
  44.8 4.9 %collective-permute-done.3.got_o = bf16[1024,128]{1,0:T(8,128)(2,1)S(1)} collective-permute-done((bf16[1024,128]{1,0:T(8,128)(2,1)S(1)}, bf16[1024,128]{1,0:T(8,128)(2,1)S(1)}, u32[]{:S(2)}, u32[]{:S(2)}) %collective-permute-start.3) | collective-permute-done | bytes 262176 | tf_op jit(solution)/shard_map/ppermute | solution.py:306
  49.7 1.0 shard_map.68
  50.7 0.1 collective-permute-start.4
  50.8 6.0 %collective-permute-start.5 = (bf16[1024,128]{1,0:T(8,128)(2,1)S(1)}, bf16[1024,128]{1,0:T(8,128)(2,1)S(1)}, u32[]{:S(2)}, u32[]{:S(2)}) collective-permute-start(bf16[1024,128]{1,0:T(8,128)(2,1)S(1)} %get-tuple-element.44), channel_id=1, source_target_pairs={{0,127},{1,2},{2,1},{3,4},{4,3},{5,6},{6,5},{7,8},{8,7},{9,10},{10... | collective-permute-start | bytes 786440 | tf_op jit(solution)/shard_map/ppermute | solution.py:306
  56.8 0.3 collective-permute-done.4.got_e
  57.1 1.1 shard_map.69.base
  58.2 6.6 %collective-permute-done.5.got_o = bf16[1024,128]{1,0:T(8,128)(2,1)S(1)} collective-permute-done((bf16[1024,128]{1,0:T(8,128)(2,1)S(1)}, bf16[1024,128]{1,0:T(8,128)(2,1)S(1)}, u32[]{:S(2)}, u32[]{:S(2)}) %collective-permute-start.5) | collective-permute-done | bytes 262176 | tf_op jit(solution)/shard_map/ppermute | solution.py:306
  64.9 1.0 shard_map.70
  65.9 0.1 collective-permute-start.6
  66.0 4.7 %collective-permute-start.7 = (bf16[1024,128]{1,0:T(8,128)(2,1)S(1)}, bf16[1024,128]{1,0:T(8,128)(2,1)S(1)}, u32[]{:S(2)}, u32[]{:S(2)}) collective-permute-start(bf16[1024,128]{1,0:T(8,128)(2,1)S(1)} %get-tuple-element.47), channel_id=1, source_target_pairs={{0,127},{1,2},{2,1},{3,4},{4,3},{5,6},{6,5},{7,8},{8,7},{9,10},{10... | collective-permute-start | bytes 786440 | tf_op jit(solution)/shard_map/ppermute | solution.py:306
  70.7 1.7 %collective-permute-done.6.got_e = bf16[1024,128]{1,0:T(8,128)(2,1)S(1)} collective-permute-done((bf16[1024,128]{1,0:T(8,128)(2,1)S(1)}, bf16[1024,128]{1,0:T(8,128)(2,1)S(1)}, u32[]{:S(2)}, u32[]{:S(2)}) %collective-permute-start.6) | collective-permute-done | bytes 262176 | tf_op jit(solution)/shard_map/ppermute | solution.py:310
  72.4 1.1 shard_map.71.base
  73.4 5.4 %collective-permute-done.7.got_o = bf16[1024,128]{1,0:T(8,128)(2,1)S(1)} collective-permute-done((bf16[1024,128]{1,0:T(8,128)(2,1)S(1)}, bf16[1024,128]{1,0:T(8,128)(2,1)S(1)}, u32[]{:S(2)}, u32[]{:S(2)}) %collective-permute-start.7) | collective-permute-done | bytes 262176 | tf_op jit(solution)/shard_map/ppermute | solution.py:306
  78.9 1.0 shard_map.72
  79.9 0.1 collective-permute-start.8
  80.0 5.1 %collective-permute-start.9 = (bf16[1024,128]{1,0:T(8,128)(2,1)S(1)}, bf16[1024,128]{1,0:T(8,128)(2,1)S(1)}, u32[]{:S(2)}, u32[]{:S(2)}) collective-permute-start(bf16[1024,128]{1,0:T(8,128)(2,1)S(1)} %get-tuple-element.50), channel_id=1, source_target_pairs={{0,127},{1,2},{2,1},{3,4},{4,3},{5,6},{6,5},{7,8},{8,7},{9,10},{10... | collective-permute-start | bytes 786440 | tf_op jit(solution)/shard_map/ppermute | solution.py:306
  85.1 1.3 %collective-permute-done.8.got_e = bf16[1024,128]{1,0:T(8,128)(2,1)S(1)} collective-permute-done((bf16[1024,128]{1,0:T(8,128)(2,1)S(1)}, bf16[1024,128]{1,0:T(8,128)(2,1)S(1)}, u32[]{:S(2)}, u32[]{:S(2)}) %collective-permute-start.8) | collective-permute-done | bytes 262176 | tf_op jit(solution)/shard_map/ppermute | solution.py:310
  86.3 1.1 shard_map.73.base
  87.4 5.0 %collective-permute-done.9.got_o = bf16[1024,128]{1,0:T(8,128)(2,1)S(1)} collective-permute-done((bf16[1024,128]{1,0:T(8,128)(2,1)S(1)}, bf16[1024,128]{1,0:T(8,128)(2,1)S(1)}, u32[]{:S(2)}, u32[]{:S(2)}) %collective-permute-start.9) | collective-permute-done | bytes 262176 | tf_op jit(solution)/shard_map/ppermute | solution.py:306
  92.4 0.7 shard_map.74
  93.1 0.1 collective-permute-start.12
  93.2 0.1 collective-permute-start.11
  93.3 4.0 %collective-permute-start.10 = (f32[128,128]{1,0:T(8,128)S(1)}, f32[128,128]{1,0:T(8,128)S(1)}, u32[]{:S(2)}, u32[]{:S(2)}) collective-permute-start(f32[128,128]{1,0:T(8,128)S(1)} %get-tuple-element.51), channel_id=1, source_target_pairs={{0,1},{1,0},{2,3},{3,2},{4,5},{5,4},{6,7},{7,6},{8,9},{9,8},{10,11... | collective-permute-start | bytes 196616 | tf_op jit(solution)/shard_map/ppermute | solution.py:322
  97.2 2.1 %collective-permute-done.12 = f32[128,128]{1,0:T(8,128)S(1)} collective-permute-done((f32[128,128]{1,0:T(8,128)S(1)}, f32[128,128]{1,0:T(8,128)S(1)}, u32[]{:S(2)}, u32[]{:S(2)}) %collective-permute-start.12) | collective-permute-done | bytes 65568 | tf_op jit(solution)/shard_map/ppermute | solution.py:322
  99.3 0.0 collective-permute-done.11
  99.3 0.9 collective-permute-done.10
  100.2 0.1 collective-permute-start.15
  100.3 0.1 collective-permute-start.14
  100.4 4.0 %collective-permute-start.13 = (f32[128,128]{1,0:T(8,128)S(1)}, f32[128,128]{1,0:T(8,128)S(1)}, u32[]{:S(2)}, u32[]{:S(2)}) collective-permute-start(f32[128,128]{1,0:T(8,128)S(1)} %add_add_fusion.2), channel_id=1, source_target_pairs={{0,4},{1,5},{2,6},{3,7},{4,0},{5,1},{6,2},{7,3},{8,12},{9,13},{10,... | collective-permute-start | bytes 196616 | tf_op jit(solution)/shard_map/ppermute | solution.py:322
  104.4 2.1 %collective-permute-done.15 = f32[128,128]{1,0:T(8,128)S(1)} collective-permute-done((f32[128,128]{1,0:T(8,128)S(1)}, f32[128,128]{1,0:T(8,128)S(1)}, u32[]{:S(2)}, u32[]{:S(2)}) %collective-permute-start.15) | collective-permute-done | bytes 65568 | tf_op jit(solution)/shard_map/ppermute | solution.py:322
  106.5 0.0 collective-permute-done.14
  106.5 0.9 collective-permute-done.13
  107.3 0.1 collective-permute-start.16
  107.4 1.2 %collective-permute-done.16 = f32[128,128]{1,0:T(8,128)S(1)} collective-permute-done((f32[128,128]{1,0:T(8,128)S(1)}, f32[128,128]{1,0:T(8,128)S(1)}, u32[]{:S(2)}, u32[]{:S(2)}) %collective-permute-start.16) | collective-permute-done | bytes 65568 | tf_op jit(solution)/shard_map/ppermute | solution.py:322
  108.7 4.4 %collective-permute-start.19 = (f32[128,128]{1,0:T(8,128)S(1)}, f32[128,128]{1,0:T(8,128)S(1)}, u32[]{:S(2)}, u32[]{:S(2)}) collective-permute-start(f32[128,128]{1,0:T(8,128)S(1)} %add.36), channel_id=1, source_target_pairs={{0,96},{1,97},{2,98},{3,99},{4,100},{5,101},{6,102},{7,103},{8,104... | collective-permute-start | bytes 196616 | tf_op jit(solution)/shard_map/ppermute | solution.py:322
  113.1 0.0 collective-permute-start.18
  113.1 0.9 collective-permute-start.17
  114.0 2.2 %collective-permute-done.19 = f32[128,128]{1,0:T(8,128)S(1)} collective-permute-done((f32[128,128]{1,0:T(8,128)S(1)}, f32[128,128]{1,0:T(8,128)S(1)}, u32[]{:S(2)}, u32[]{:S(2)}) %collective-permute-start.19) | collective-permute-done | bytes 65568 | tf_op jit(solution)/shard_map/ppermute | solution.py:322
  116.2 3.0 %collective-permute-done.18 = f32[128,128]{1,0:T(8,128)S(1)} collective-permute-done((f32[128,128]{1,0:T(8,128)S(1)}, f32[128,128]{1,0:T(8,128)S(1)}, u32[]{:S(2)}, u32[]{:S(2)}) %collective-permute-start.18) | collective-permute-done | bytes 65568 | tf_op jit(solution)/shard_map/ppermute | solution.py:322
  119.1 0.0 collective-permute-done.17
  119.2 4.3 %shard_map.75 = f32[1024,128]{1,0:T(8,128)} custom-call(f32[128,128]{1,0:T(8,128)S(1)} %add_add_fusion.gram, bf16[1024,128]{1,0:T(8,128)(2,1)S(1)} %get-tuple-element.52.y), custom_call_target="tpu_custom_call" | custom-call | flops 536870912 | bytes 1000000 | tf_op jit(solution)/shard_map/pallas_call | solution.py:386
  (7 shorter events, 0.1 us)
Async XLA Ops:
  0.0 16.2 %copy-start.2 = (bf16[1024,128]{1,0:T(8,128)(2,1)S(1)}, bf16[1024,128]{1,0:T(8,128)(2,1)}, u32[]{:S(2)}) copy-start(bf16[1024,128]{1,0:T(8,128)(2,1)} %older.1) | copy-start | bytes 786436
  0.0 16.0 %copy-start.6 = (f32[1024]{0:T(1024)S(1)}, f32[1024]{0:T(1024)}, u32[]{:S(2)}) copy-start(f32[1024]{0:T(1024)} %param.10) | copy-start | bytes 12292
  7.2 19.2 %collective-permute-start = (bf16[3072,128]{1,0:T(8,128)(2,1)}, bf16[3072,128]{1,0:T(8,128)(2,1)S(1)}, u32[]{:S(2)}, u32[]{:S(2)}) collective-permute-start(bf16[3072,128]{1,0:T(8,128)(2,1)} %get-tuple-element.35.to_e), channel_id=1, source_target_pairs={{0,1},{1,0},{2,3},{3,2},{4,5},{5,4},{6,7},{7,6},{8,9},{9,8},{10,11... | collective-permute-start | bytes 2359304 | tf_op jit(solution)/shard_map/ppermute | solution.py:310
  8.5 25.1 %collective-permute-start.1 = (bf16[3072,128]{1,0:T(8,128)(2,1)}, bf16[3072,128]{1,0:T(8,128)(2,1)S(1)}, u32[]{:S(2)}, u32[]{:S(2)}) collective-permute-start(bf16[3072,128]{1,0:T(8,128)(2,1)} %get-tuple-element.36.to_o), channel_id=1, source_target_pairs={{0,127},{1,2},{2,1},{3,4},{4,3},{5,6},{6,5},{7,8},{8,7},{9,10},{10... | collective-permute-start | bytes 2359304 | tf_op jit(solution)/shard_map/ppermute | solution.py:306
  16.2 1.6 %copy-start = (bf16[1024,1024]{1,0:T(8,128)(2,1)S(1)}, bf16[1024,1024]{1,0:T(8,128)(2,1)}, u32[]{:S(2)}) copy-start(bf16[1024,1024]{1,0:T(8,128)(2,1)} %get-tuple-element.30.edge.edge_in) | copy-start | bytes 6291460
  17.8 1.6 %copy-start.3 = (bf16[1024,1024]{1,0:T(8,128)(2,1)S(1)}, bf16[1024,1024]{1,0:T(8,128)(2,1)}, u32[]{:S(2)}) copy-start(bf16[1024,1024]{1,0:T(8,128)(2,1)} %get-tuple-element.29.own) | copy-start | bytes 6291460
  19.4 14.2 %copy-start.1 = (bf16[1024,1024]{1,0:T(8,128)(2,1)S(1)}, bf16[1024,1024]{1,0:T(8,128)(2,1)}, u32[]{:S(2)}) copy-start(bf16[1024,1024]{1,0:T(8,128)(2,1)} %get-tuple-element.30.edge.edge_in) | copy-start | bytes 6291460
  19.4 14.2 %copy-start.4 = (bf16[3072,128]{1,0:T(8,128)(2,1)S(1)}, bf16[3072,128]{1,0:T(8,128)(2,1)}, u32[]{:S(2)}) copy-start(bf16[3072,128]{1,0:T(8,128)(2,1)} %get-tuple-element.35.to_e) | copy-start | bytes 2359300
  19.4 14.2 %copy-start.5 = (bf16[3072,128]{1,0:T(8,128)(2,1)S(1)}, bf16[3072,128]{1,0:T(8,128)(2,1)}, u32[]{:S(2)}) copy-start(bf16[3072,128]{1,0:T(8,128)(2,1)} %get-tuple-element.36.to_o) | copy-start | bytes 2359300
  35.8 7.9 %collective-permute-start.2 = (bf16[1024,128]{1,0:T(8,128)(2,1)S(1)}, bf16[1024,128]{1,0:T(8,128)(2,1)S(1)}, u32[]{:S(2)}, u32[]{:S(2)}) collective-permute-start(bf16[1024,128]{1,0:T(8,128)(2,1)S(1)} %get-tuple-element.39), channel_id=1, source_target_pairs={{0,1},{1,0},{2,3},{3,2},{4,5},{5,4},{6,7},{7,6},{8,9},{9,8},{10,11... | collective-permute-start | bytes 786440 | tf_op jit(solution)/shard_map/ppermute | solution.py:310
  35.9 13.8 %collective-permute-start.3 = (bf16[1024,128]{1,0:T(8,128)(2,1)S(1)}, bf16[1024,128]{1,0:T(8,128)(2,1)S(1)}, u32[]{:S(2)}, u32[]{:S(2)}) collective-permute-start(bf16[1024,128]{1,0:T(8,128)(2,1)S(1)} %get-tuple-element.41), channel_id=1, source_target_pairs={{0,127},{1,2},{2,1},{3,4},{4,3},{5,6},{6,5},{7,8},{8,7},{9,10},{10... | collective-permute-start | bytes 786440 | tf_op jit(solution)/shard_map/ppermute | solution.py:306
  50.7 6.5 %collective-permute-start.4 = (bf16[1024,128]{1,0:T(8,128)(2,1)S(1)}, bf16[1024,128]{1,0:T(8,128)(2,1)S(1)}, u32[]{:S(2)}, u32[]{:S(2)}) collective-permute-start(bf16[1024,128]{1,0:T(8,128)(2,1)S(1)} %get-tuple-element.43), channel_id=1, source_target_pairs={{0,1},{1,0},{2,3},{3,2},{4,5},{5,4},{6,7},{7,6},{8,9},{9,8},{10,11... | collective-permute-start | bytes 786440 | tf_op jit(solution)/shard_map/ppermute | solution.py:310
  50.8 14.1 %collective-permute-start.5 = (bf16[1024,128]{1,0:T(8,128)(2,1)S(1)}, bf16[1024,128]{1,0:T(8,128)(2,1)S(1)}, u32[]{:S(2)}, u32[]{:S(2)}) collective-permute-start(bf16[1024,128]{1,0:T(8,128)(2,1)S(1)} %get-tuple-element.44), channel_id=1, source_target_pairs={{0,127},{1,2},{2,1},{3,4},{4,3},{5,6},{6,5},{7,8},{8,7},{9,10},{10... | collective-permute-start | bytes 786440 | tf_op jit(solution)/shard_map/ppermute | solution.py:306
  65.9 6.5 %collective-permute-start.6 = (bf16[1024,128]{1,0:T(8,128)(2,1)S(1)}, bf16[1024,128]{1,0:T(8,128)(2,1)S(1)}, u32[]{:S(2)}, u32[]{:S(2)}) collective-permute-start(bf16[1024,128]{1,0:T(8,128)(2,1)S(1)} %get-tuple-element.46), channel_id=1, source_target_pairs={{0,1},{1,0},{2,3},{3,2},{4,5},{5,4},{6,7},{7,6},{8,9},{9,8},{10,11... | collective-permute-start | bytes 786440 | tf_op jit(solution)/shard_map/ppermute | solution.py:310
  66.0 12.9 %collective-permute-start.7 = (bf16[1024,128]{1,0:T(8,128)(2,1)S(1)}, bf16[1024,128]{1,0:T(8,128)(2,1)S(1)}, u32[]{:S(2)}, u32[]{:S(2)}) collective-permute-start(bf16[1024,128]{1,0:T(8,128)(2,1)S(1)} %get-tuple-element.47), channel_id=1, source_target_pairs={{0,127},{1,2},{2,1},{3,4},{4,3},{5,6},{6,5},{7,8},{8,7},{9,10},{10... | collective-permute-start | bytes 786440 | tf_op jit(solution)/shard_map/ppermute | solution.py:306
  79.9 6.5 %collective-permute-start.8 = (bf16[1024,128]{1,0:T(8,128)(2,1)S(1)}, bf16[1024,128]{1,0:T(8,128)(2,1)S(1)}, u32[]{:S(2)}, u32[]{:S(2)}) collective-permute-start(bf16[1024,128]{1,0:T(8,128)(2,1)S(1)} %get-tuple-element.49), channel_id=1, source_target_pairs={{0,1},{1,0},{2,3},{3,2},{4,5},{5,4},{6,7},{7,6},{8,9},{9,8},{10,11... | collective-permute-start | bytes 786440 | tf_op jit(solution)/shard_map/ppermute | solution.py:310
  80.0 12.4 %collective-permute-start.9 = (bf16[1024,128]{1,0:T(8,128)(2,1)S(1)}, bf16[1024,128]{1,0:T(8,128)(2,1)S(1)}, u32[]{:S(2)}, u32[]{:S(2)}) collective-permute-start(bf16[1024,128]{1,0:T(8,128)(2,1)S(1)} %get-tuple-element.50), channel_id=1, source_target_pairs={{0,127},{1,2},{2,1},{3,4},{4,3},{5,6},{6,5},{7,8},{8,7},{9,10},{10... | collective-permute-start | bytes 786440 | tf_op jit(solution)/shard_map/ppermute | solution.py:306
  93.1 6.3 %collective-permute-start.12 = (f32[128,128]{1,0:T(8,128)S(1)}, f32[128,128]{1,0:T(8,128)S(1)}, u32[]{:S(2)}, u32[]{:S(2)}) collective-permute-start(f32[128,128]{1,0:T(8,128)S(1)} %get-tuple-element.51), channel_id=1, source_target_pairs={{0,3},{1,2},{2,1},{3,0},{4,7},{5,6},{6,5},{7,4},{8,11},{9,10},{10,... | collective-permute-start | bytes 196616 | tf_op jit(solution)/shard_map/ppermute | solution.py:322
  93.2 6.2 %collective-permute-start.11 = (f32[128,128]{1,0:T(8,128)S(1)}, f32[128,128]{1,0:T(8,128)S(1)}, u32[]{:S(2)}, u32[]{:S(2)}) collective-permute-start(f32[128,128]{1,0:T(8,128)S(1)} %get-tuple-element.51), channel_id=1, source_target_pairs={{0,2},{1,3},{2,0},{3,1},{4,6},{5,7},{6,4},{7,5},{8,10},{9,11},{10,... | collective-permute-start | bytes 196616 | tf_op jit(solution)/shard_map/ppermute | solution.py:322
  93.3 6.9 %collective-permute-start.10 = (f32[128,128]{1,0:T(8,128)S(1)}, f32[128,128]{1,0:T(8,128)S(1)}, u32[]{:S(2)}, u32[]{:S(2)}) collective-permute-start(f32[128,128]{1,0:T(8,128)S(1)} %get-tuple-element.51), channel_id=1, source_target_pairs={{0,1},{1,0},{2,3},{3,2},{4,5},{5,4},{6,7},{7,6},{8,9},{9,8},{10,11... | collective-permute-start | bytes 196616 | tf_op jit(solution)/shard_map/ppermute | solution.py:322
  100.2 6.3 %collective-permute-start.15 = (f32[128,128]{1,0:T(8,128)S(1)}, f32[128,128]{1,0:T(8,128)S(1)}, u32[]{:S(2)}, u32[]{:S(2)}) collective-permute-start(f32[128,128]{1,0:T(8,128)S(1)} %add_add_fusion.2), channel_id=1, source_target_pairs={{0,12},{1,13},{2,14},{3,15},{4,8},{5,9},{6,10},{7,11},{8,4},{9,5},... | collective-permute-start | bytes 196616 | tf_op jit(solution)/shard_map/ppermute | solution.py:322
  100.3 6.2 %collective-permute-start.14 = (f32[128,128]{1,0:T(8,128)S(1)}, f32[128,128]{1,0:T(8,128)S(1)}, u32[]{:S(2)}, u32[]{:S(2)}) collective-permute-start(f32[128,128]{1,0:T(8,128)S(1)} %add_add_fusion.2), channel_id=1, source_target_pairs={{0,8},{1,9},{2,10},{3,11},{4,12},{5,13},{6,14},{7,15},{8,0},{9,1},... | collective-permute-start | bytes 196616 | tf_op jit(solution)/shard_map/ppermute | solution.py:322
  100.4 6.9 %collective-permute-start.13 = (f32[128,128]{1,0:T(8,128)S(1)}, f32[128,128]{1,0:T(8,128)S(1)}, u32[]{:S(2)}, u32[]{:S(2)}) collective-permute-start(f32[128,128]{1,0:T(8,128)S(1)} %add_add_fusion.2), channel_id=1, source_target_pairs={{0,4},{1,5},{2,6},{3,7},{4,0},{5,1},{6,2},{7,3},{8,12},{9,13},{10,... | collective-permute-start | bytes 196616 | tf_op jit(solution)/shard_map/ppermute | solution.py:322
  107.3 1.3 %collective-permute-start.16 = (f32[128,128]{1,0:T(8,128)S(1)}, f32[128,128]{1,0:T(8,128)S(1)}, u32[]{:S(2)}, u32[]{:S(2)}) collective-permute-start(f32[128,128]{1,0:T(8,128)S(1)} %add_add_fusion.1), channel_id=1, source_target_pairs={{0,16},{1,17},{2,18},{3,19},{4,20},{5,21},{6,22},{7,23},{8,24},{9,... | collective-permute-start | bytes 196616 | tf_op jit(solution)/shard_map/ppermute | solution.py:322
  108.7 7.5 %collective-permute-start.19 = (f32[128,128]{1,0:T(8,128)S(1)}, f32[128,128]{1,0:T(8,128)S(1)}, u32[]{:S(2)}, u32[]{:S(2)}) collective-permute-start(f32[128,128]{1,0:T(8,128)S(1)} %add.36), channel_id=1, source_target_pairs={{0,96},{1,97},{2,98},{3,99},{4,100},{5,101},{6,102},{7,103},{8,104... | collective-permute-start | bytes 196616 | tf_op jit(solution)/shard_map/ppermute | solution.py:322
  113.1 6.1 %collective-permute-start.18 = (f32[128,128]{1,0:T(8,128)S(1)}, f32[128,128]{1,0:T(8,128)S(1)}, u32[]{:S(2)}, u32[]{:S(2)}) collective-permute-start(f32[128,128]{1,0:T(8,128)S(1)} %add.36), channel_id=1, source_target_pairs={{0,64},{1,65},{2,66},{3,67},{4,68},{5,69},{6,70},{7,71},{8,72},{9,... | collective-permute-start | bytes 196616 | tf_op jit(solution)/shard_map/ppermute | solution.py:322
  113.1 6.1 %collective-permute-start.17 = (f32[128,128]{1,0:T(8,128)S(1)}, f32[128,128]{1,0:T(8,128)S(1)}, u32[]{:S(2)}, u32[]{:S(2)}) collective-permute-start(f32[128,128]{1,0:T(8,128)S(1)} %add.36), channel_id=1, source_target_pairs={{0,32},{1,33},{2,34},{3,35},{4,36},{5,37},{6,38},{7,39},{8,40},{9,... | collective-permute-start | bytes 196616 | tf_op jit(solution)/shard_map/ppermute | solution.py:322
where the time goes:
time: 122 us; the launch traced here: 123 us
  waiting for transfers between devices  50.7 us (42%)
  starting transfers between devices  45.7 us (37%)
  Pallas kernels  23.3 us (19%)
  local copies, waits for them, and re-layouts  3.41 us (3%)
    ppermute x5, starting transfers between devices, swap_o(): lax.ppermute(value, AXES, [(i, (i + 1 if i % 2 else i - 1) % count) for i...  30.4 us
    ppermute x5, waiting for transfers between devices, swap_o(): lax.ppermute(value, AXES, [(i, (i + 1 if i % 2 else i - 1) % count) for i...  29.1 us
    ppermute x10, starting transfers between devices, group_sum(): parts.append(lax.ppermute(value, AXES, pairs))  13.7 us
    ppermute x10, waiting for transfers between devices, group_sum(): parts.append(lax.ppermute(value, AXES, pairs))  12.3 us
    ppermute x5, waiting for transfers between devices, swap_e(): lax.ppermute(value, AXES, [(i, i ^ 1) for i in range(lax.axis_size(AXES))])  9.37 us
    pallas_call x1, Pallas kernels, local(): call(functools.partial(prep_kernel, total), [square, square, message, mes...  7.24 us
    pallas_call x4, Pallas kernels, local(): call(local_kernel, [tall32], [VMEM] * 6, product, 3500000)  4.35 us
    pallas_call x1, Pallas kernels, local(): call(functools.partial(finish_kernel, scale), [tall32], [VMEM] * 2, 2 * p...  4.27 us
  transfers between devices with their start and end apart: 20, of which 17 were waited for; matrix products, arithmetic and copies ran while one was open for 0% of the time, Pallas kernels for 5%

commit v1 on v0

--- a/solution.py
+++ b/solution.py
@@ -43,11 +43,22 @@
     return block.astype(F32).T
 
 
-def prep_kernel(total, scales, columns, live, blocks, y0, own, edge, to_e, to_o, buf, acc, head, after, sem):
+def prep_kernel(total, scales_in, columns_in, live_in, blocks, y0, own_out, edge_out, to_e, to_o, buf, acc, own, edge, msg, y0_in, scales, columns, live, head, after, sem, sent):
+    small = [
+        pltpu.make_async_copy(source, target, sent.at[15 + i])
+        for i, (source, target) in enumerate(((live_in, live), (columns_in, columns), (scales_in, scales)))
+    ]
+    for copy in small:
+        copy.start()
+    start_y0 = pltpu.make_async_copy(y0, y0_in, sent.at[12])
+    start_y0.start()
     copies = [pltpu.make_async_copy(blocks.at[a], buf.at[a], sem.at[a]) for a in range(ROWS)]
     for copy in copies:
         copy.start()
+    even = lax.rem(lax.axis_index(AXES), 2) == 0
     first = lax.axis_index(AXES) * ROWS
+    for copy in small:
+        copy.wait()
     for a in range(ROWS):
         for o in range(SPAN):
             head[a, o] = -1
@@ -59,17 +70,27 @@
             return carry
 
         lax.fori_loop(0, live[a], chain, 0)
-    turned = flip(y0[...]).astype(BF16)
-    for target in (to_e, to_o):
-        target[pl.ds(HANDED + 2 * B, OWN), :] = y0[...]
-    even = lax.rem(lax.axis_index(AXES), 2) == 0
-
-    def put_message(right, start, value):
-        for case, target in ((even, to_e if right else to_o), (~even, to_o if right else to_e)):
-
-            @pl.when(case)
-            def _(target=target):
-                target[pl.ds(start, value.shape[0]), :] = value
+    start_y0.wait()
+    waits = []
+    for i, target in enumerate((to_e, to_o)):
+        copy = pltpu.make_async_copy(y0_in, target.at[pl.ds(HANDED + 2 * B, OWN), :], sent.at[10 + i])
+        copy.start()
+        waits.append(copy)
+    turned = flip(y0_in[...]).astype(BF16)
+
+    def post_message(right, start, count, slot):
+        side = 0 if right else 1
+        part = pl.ds(start, count)
+
+        @pl.when(even == right)
+        def _():
+            pltpu.make_async_copy(msg.at[side, part, :], to_e.at[part, :], sent.at[slot]).start()
+
+        @pl.when(even != right)
+        def _():
+            pltpu.make_async_copy(msg.at[side, part, :], to_o.at[part, :], sent.at[slot]).start()
+
+        waits.append(pltpu.make_async_copy(msg.at[side, part, :], to_e.at[part, :], sent.at[slot]))
 
     def put(a, p, value):
         if 4 <= p < 8:
@@ -77,10 +98,10 @@
         elif p in EDGE:
             edge[rows(a), rows(EDGE.index(p))] = value
         else:
-            right = p > 8
-            i = (TO_RIGHT if right else TO_LEFT).index((a, p))
-            put_message(right, 2 * i * B, value[:, :K])
-            put_message(right, (2 * i + 1) * B, value[:, K:])
+            side, places = (0, TO_RIGHT) if p > 8 else (1, TO_LEFT)
+            i = places.index((a, p))
+            msg[side, rows(2 * i), :] = value[:, :K]
+            msg[side, rows(2 * i + 1), :] = value[:, K:]
 
     def scaled(a, s):
         return (scales[a, s] * ALPHA) * buf[a, s].astype(F32)
@@ -100,7 +121,13 @@
             def _():
                 put(a, a + o, scaled(a, s).astype(BF16))
 
-            @pl.when(rest >= 0)
+            last = after[a, jnp.maximum(rest, 0)]
+
+            @pl.when((rest >= 0) & (last < 0))
+            def _():
+                put(a, a + o, (scaled(a, s) + scaled(a, rest)).astype(BF16))
+
+            @pl.when((rest >= 0) & (last >= 0))
             def _():
                 acc[...] = scaled(a, s)
 
@@ -117,9 +144,19 @@
         copies[a].wait()
         for o in range(SPAN):
             place(a, o)
+        for i, (source, target) in enumerate(((own, own_out), (edge, edge_out))):
+            copy = pltpu.make_async_copy(source.at[rows(a), :], target.at[rows(a), :], sent.at[4 * i + a])
+            copy.start()
+            waits.append(copy)
+        if a % 2 == 1:
+            post_message(a == 3, 0, HANDED, 8 if a == 3 else 9)
     terms = dot(turned, edge[...]).T.astype(BF16)
-    put_message(True, HANDED, terms[: 2 * B])
-    put_message(False, HANDED, terms[2 * B :])
+    msg[0, pl.ds(HANDED, 2 * B), :] = terms[: 2 * B]
+    msg[1, pl.ds(HANDED, 2 * B), :] = terms[2 * B :]
+    post_message(True, HANDED, 2 * B, 13)
+    post_message(False, HANDED, 2 * B, 14)
+    for copy in waits:
+        copy.wait()
 
 
 def first_local_kernel(own, edge, onsite, y0, diag, sym, edge_t, base):
@@ -288,12 +325,12 @@
 PREP_LIMIT = 57 * 1000 * 1000
 
 
-def call(kernel, outs, specs, flops, size, scratch=(), aliases=None, limit=LIMIT):
+def call(kernel, outs, specs, flops, size, scratch=(), aliases=None, limit=LIMIT, out_spec=None):
     return pl.pallas_call(
         kernel,
         out_shape=[jax.ShapeDtypeStruct(*out) for out in outs],
         in_specs=list(specs),
-        out_specs=[VMEM] * len(outs),
+        out_specs=[out_spec or VMEM] * len(outs),
         scratch_shapes=list(scratch),
         input_output_aliases=aliases or {},
         cost_estimate=pl.CostEstimate(flops=flops, bytes_accessed=size, transcendentals=0),
@@ -350,16 +387,25 @@
     own, edge, to_e, to_o = call(
         functools.partial(prep_kernel, total),
         [square, square, message, message],
-        [SMEM, SMEM, SMEM, HBM, VMEM],
+        [HBM] * 5,
         product,
         10_000_000,
         [
             pltpu.VMEM((ROWS, slots, B, B), BF16),
             pltpu.VMEM((B, B), F32),
+            pltpu.VMEM((OWN, OWN), BF16),
+            pltpu.VMEM((OWN, OWN), BF16),
+            pltpu.VMEM((2, HANDED + 2 * B, K), BF16),
+            pltpu.VMEM((OWN, K), BF16),
+            pltpu.SMEM((ROWS, slots), F32),
+            pltpu.SMEM((ROWS, slots), jnp.int32),
+            pltpu.SMEM((ROWS,), jnp.int32),
             pltpu.SMEM((ROWS, SPAN), jnp.int32),
             pltpu.SMEM((ROWS, slots), jnp.int32),
             pltpu.SemaphoreType.DMA((ROWS,)),
+            pltpu.SemaphoreType.DMA((18,)),
         ],
+        out_spec=HBM,
         limit=PREP_LIMIT,
     )(block_scales, columns, live, blocks, y0)
     got_o, got_e = swap_o(to_o), swap_e(to_e)

time: 122 us -> 120 us (0.984); the launches traced: 123 us -> 120 us
  Pallas kernels: 23.3 us -> 21.7 us
  starting transfers between devices: 45.7 us -> 44.4 us
    pallas_call x1, Pallas kernels: 7.24 us -> 5.25 us  [local(): call(functools.partial(prep_kernel, total), [square, square, message, mes...]
    ppermute x10, waiting for transfers between devices: 12.3 us -> 10.5 us  [group_sum(): parts.append(lax.ppermute(value, AXES, pairs))]
    ppermute x5, waiting for transfers between devices: 9.37 us -> 10.7 us  [swap_e(): lax.ppermute(value, AXES, [(i, i ^ 1) for i in range(lax.axis_size(AXES))])]
where the time goes in v1:
time: 120 us
  waiting for transfers between devices  49.9 us (42%)
  starting transfers between devices  44.4 us (37%)
  Pallas kernels  21.7 us (18%)
  local copies, waits for them, and re-layouts  3.41 us (3%)
    ppermute x5, starting transfers between devices, swap_o(): lax.ppermute(value, AXES, [(i, (i + 1 if i % 2 else i - 1) % count) for i...  29.7 us
    ppermute x5, waiting for transfers between devices, swap_o(): lax.ppermute(value, AXES, [(i, (i + 1 if i % 2 else i - 1) % count) for i...  28.8 us
    ppermute x10, starting transfers between devices, group_sum(): parts.append(lax.ppermute(value, AXES, pairs))  12.6 us
    ppermute x5, waiting for transfers between devices, swap_e(): lax.ppermute(value, AXES, [(i, i ^ 1) for i in range(lax.axis_size(AXES))])  10.7 us
    ppermute x10, waiting for transfers between devices, group_sum(): parts.append(lax.ppermute(value, AXES, pairs))  10.5 us
    pallas_call x1, Pallas kernels, local(): call(functools.partial(prep_kernel, total), [square, square, message, mes...  5.25 us
    pallas_call x4, Pallas kernels, local(): call(local_kernel, [tall32], [VMEM] * 6, product, 3500000)  4.34 us
    pallas_call x1, Pallas kernels, local(): call(functools.partial(finish_kernel, scale), [tall32], [VMEM] * 2, 2 * p...  4.27 us
  transfers between devices with their start and end apart: 20, of which 17 were waited for; matrix products, arithmetic and copies ran while one was open for 0% of the time, Pallas kernels for 5%

profile of v1, /device:TPU:0, one launch (start us, length us, event | category | flops | bytes accessed | tf_op | source)
XLA Modules:
  0.0 119.8 jit_solution(176923932693569285)
XLA Ops:
  0.0 0.0 copy-start.2
  0.0 0.0 copy-start.6
  0.0 5.3 %shard_map.64 = (bf16[1024,1024]{1,0:T(8,128)(2,1)}, bf16[1024,1024]{1,0:T(8,128)(2,1)}, bf16[3072,128]{1,0:T(8,128)(2,1)}, bf16[3072,128]{1,0:T(8,128)(2,1)}) custom-call(f32[4,10]{1,0:T(4,128)} %scales_in.1, s32[4,10]{1,0:T(4,128)} %columns_in.1, s32[4]{0:T(128)} %live_in.1, bf16[4,10,256,256]{3,2,1,0:T(8,128)(2,1)} %blocks.1, bf16[1024,128]{1,0:T(8,128)(2,1)} %older.1), custom_call_target="tpu_custom_call" | custom-call | flops 268435456 | bytes 10000000 | tf_op jit(solution)/shard_map/pallas_call | solution.py:387
  5.3 1.9 %collective-permute-start = (bf16[3072,128]{1,0:T(8,128)(2,1)}, bf16[3072,128]{1,0:T(8,128)(2,1)S(1)}, u32[]{:S(2)}, u32[]{:S(2)}) collective-permute-start(bf16[3072,128]{1,0:T(8,128)(2,1)} %get-tuple-element.35.to_e), channel_id=1, source_target_pairs={{0,1},{1,0},{2,3},{3,2},{4,5},{5,4},{6,7},{7,6},{8,9},{9,8},{10,11... | collective-permute-start | bytes 2359304 | tf_op jit(solution)/shard_map/ppermute | solution.py:347
  7.1 7.5 %collective-permute-start.1 = (bf16[3072,128]{1,0:T(8,128)(2,1)}, bf16[3072,128]{1,0:T(8,128)(2,1)S(1)}, u32[]{:S(2)}, u32[]{:S(2)}) collective-permute-start(bf16[3072,128]{1,0:T(8,128)(2,1)} %get-tuple-element.36.to_o), channel_id=1, source_target_pairs={{0,127},{1,2},{2,1},{3,4},{4,3},{5,6},{6,5},{7,8},{8,7},{9,10},{10... | collective-permute-start | bytes 2359304 | tf_op jit(solution)/shard_map/ppermute | solution.py:343
  14.7 0.0 copy-done.6
  14.7 0.2 copy.9.onsite
  14.9 0.0 copy-done.2
  14.9 0.0 copy-start
  14.9 1.6 %copy-done = bf16[1024,1024]{1,0:T(8,128)(2,1)S(1)} copy-done((bf16[1024,1024]{1,0:T(8,128)(2,1)S(1)}, bf16[1024,1024]{1,0:T(8,128)(2,1)}, u32[]{:S(2)}) %copy-start) | copy-done | bytes 2097176
  16.5 0.0 copy-start.3
  16.5 1.6 %copy-done.3 = bf16[1024,1024]{1,0:T(8,128)(2,1)S(1)} copy-done((bf16[1024,1024]{1,0:T(8,128)(2,1)S(1)}, bf16[1024,1024]{1,0:T(8,128)(2,1)}, u32[]{:S(2)}) %copy-start.3) | copy-done | bytes 2097176
  18.1 1.6 %shard_map.65 = (f32[1024,1]{1,0:T(8,128)S(1)}, bf16[1024,1024]{1,0:T(8,128)(2,1)S(1)}, bf16[1024,1024]{1,0:T(8,128)(2,1)S(1)}, f32[1024,128]{1,0:T(8,128)S(1)}) custom-call(bf16[1024,1024]{1,0:T(8,128)(2,1)S(1)} %copy-done.3, bf16[1024,1024]{1,0:T(8,128)(2,1)S(1)} %copy-done, f32[1024,1]{1,0:T(8,128)S(1)} %copy.9.onsite, bf16[1024,128]{1,0:T(8,128)(2,1)S(1)} %copy-done.2), custom_call_target="tpu_custom_call" | custom-call | flops 268435456 | bytes 10000000 | tf_op jit(solution)/shard_map/pallas_call | solution.py:412
  19.7 5.0 %collective-permute-done.got_e = bf16[3072,128]{1,0:T(8,128)(2,1)S(1)} collective-permute-done((bf16[3072,128]{1,0:T(8,128)(2,1)}, bf16[3072,128]{1,0:T(8,128)(2,1)S(1)}, u32[]{:S(2)}, u32[]{:S(2)}) %collective-permute-start) | collective-permute-done | bytes 786464 | tf_op jit(solution)/shard_map/ppermute | solution.py:347
  24.8 7.4 %collective-permute-done.1.got_o = bf16[3072,128]{1,0:T(8,128)(2,1)S(1)} collective-permute-done((bf16[3072,128]{1,0:T(8,128)(2,1)}, bf16[3072,128]{1,0:T(8,128)(2,1)S(1)}, u32[]{:S(2)}, u32[]{:S(2)}) %collective-permute-start.1) | collective-permute-done | bytes 786464 | tf_op jit(solution)/shard_map/ppermute | solution.py:343
  32.1 0.0 copy-done.1
  32.2 0.0 copy-done.4
  32.2 0.0 copy-done.5
  32.2 2.3 %shard_map.66 = (bf16[1024,1024]{1,0:T(8,128)(2,1)S(1)}, bf16[1024,1024]{1,0:T(8,128)(2,1)S(1)}, bf16[1024,128]{1,0:T(8,128)(2,1)S(1)}, bf16[1024,128]{1,0:T(8,128)(2,1)S(1)}, bf16[1024,128]{1,0:T(8,128)(2,1)S(1)}) custom-call(f32[1024,128]{1,0:T(8,128)S(1)} %get-tuple-element.33.base, ...), custom_call_target="tpu_custom_call", output_to_operand_aliasing={{0}: (1, {}), {1}: (2, {})} | custom-call | flops 536870912 | bytes 9000000 | tf_op jit(solution)/shard_map/pallas_call | solution.py:415
  34.5 0.1 collective-permute-start.2
  34.6 6.9 %collective-permute-start.3 = (bf16[1024,128]{1,0:T(8,128)(2,1)S(1)}, bf16[1024,128]{1,0:T(8,128)(2,1)S(1)}, u32[]{:S(2)}, u32[]{:S(2)}) collective-permute-start(bf16[1024,128]{1,0:T(8,128)(2,1)S(1)} %get-tuple-element.41), channel_id=1, source_target_pairs={{0,127},{1,2},{2,1},{3,4},{4,3},{5,6},{6,5},{7,8},{8,7},{9,10},{10... | collective-permute-start | bytes 786440 | tf_op jit(solution)/shard_map/ppermute | solution.py:343
  41.5 0.4 collective-permute-done.2.got_e
  41.9 1.1 shard_map.67.base
  43.0 5.1 %collective-permute-done.3.got_o = bf16[1024,128]{1,0:T(8,128)(2,1)S(1)} collective-permute-done((bf16[1024,128]{1,0:T(8,128)(2,1)S(1)}, bf16[1024,128]{1,0:T(8,128)(2,1)S(1)}, u32[]{:S(2)}, u32[]{:S(2)}) %collective-permute-start.3) | collective-permute-done | bytes 262176 | tf_op jit(solution)/shard_map/ppermute | solution.py:343
  48.1 1.0 shard_map.68
  49.1 0.1 collective-permute-start.4
  49.2 6.1 %collective-permute-start.5 = (bf16[1024,128]{1,0:T(8,128)(2,1)S(1)}, bf16[1024,128]{1,0:T(8,128)(2,1)S(1)}, u32[]{:S(2)}, u32[]{:S(2)}) collective-permute-start(bf16[1024,128]{1,0:T(8,128)(2,1)S(1)} %get-tuple-element.44), channel_id=1, source_target_pairs={{0,127},{1,2},{2,1},{3,4},{4,3},{5,6},{6,5},{7,8},{8,7},{9,10},{10... | collective-permute-start | bytes 786440 | tf_op jit(solution)/shard_map/ppermute | solution.py:343
  55.3 0.2 collective-permute-done.4.got_e
  55.6 1.1 shard_map.69.base
  56.7 6.5 %collective-permute-done.5.got_o = bf16[1024,128]{1,0:T(8,128)(2,1)S(1)} collective-permute-done((bf16[1024,128]{1,0:T(8,128)(2,1)S(1)}, bf16[1024,128]{1,0:T(8,128)(2,1)S(1)}, u32[]{:S(2)}, u32[]{:S(2)}) %collective-permute-start.5) | collective-permute-done | bytes 262176 | tf_op jit(solution)/shard_map/ppermute | solution.py:343
  63.2 1.0 shard_map.70
  64.2 0.1 collective-permute-start.6
  64.3 5.1 %collective-permute-start.7 = (bf16[1024,128]{1,0:T(8,128)(2,1)S(1)}, bf16[1024,128]{1,0:T(8,128)(2,1)S(1)}, u32[]{:S(2)}, u32[]{:S(2)}) collective-permute-start(bf16[1024,128]{1,0:T(8,128)(2,1)S(1)} %get-tuple-element.47), channel_id=1, source_target_pairs={{0,127},{1,2},{2,1},{3,4},{4,3},{5,6},{6,5},{7,8},{8,7},{9,10},{10... | collective-permute-start | bytes 786440 | tf_op jit(solution)/shard_map/ppermute | solution.py:343
  69.5 1.2 %collective-permute-done.6.got_e = bf16[1024,128]{1,0:T(8,128)(2,1)S(1)} collective-permute-done((bf16[1024,128]{1,0:T(8,128)(2,1)S(1)}, bf16[1024,128]{1,0:T(8,128)(2,1)S(1)}, u32[]{:S(2)}, u32[]{:S(2)}) %collective-permute-start.6) | collective-permute-done | bytes 262176 | tf_op jit(solution)/shard_map/ppermute | solution.py:347
  70.7 1.1 shard_map.71.base
  71.8 7.2 %collective-permute-done.7.got_o = bf16[1024,128]{1,0:T(8,128)(2,1)S(1)} collective-permute-done((bf16[1024,128]{1,0:T(8,128)(2,1)S(1)}, bf16[1024,128]{1,0:T(8,128)(2,1)S(1)}, u32[]{:S(2)}, u32[]{:S(2)}) %collective-permute-start.7) | collective-permute-done | bytes 262176 | tf_op jit(solution)/shard_map/ppermute | solution.py:343
  79.0 1.2 %shard_map.72 = (bf16[1024,128]{1,0:T(8,128)(2,1)S(1)}, bf16[1024,128]{1,0:T(8,128)(2,1)S(1)}, bf16[1024,128]{1,0:T(8,128)(2,1)S(1)}) custom-call(f32[1024,128]{1,0:T(8,128)S(1)} %shard_map.71.base, bf16[1024,1024]{1,0:T(8,128)(2,1)S(1)} %get-tuple-element.38.edge, bf16[1024,1024]{1,0:T(8,128)(2,1)S(1)} %get-tuple-element.40.edge_t, ...), custom_call_target="tpu_custom_call" | custom-call | flops 536870912 | bytes 6000000 | tf_op jit(solution)/shard_map/pallas_call | solution.py:424
  80.3 0.1 collective-permute-start.8
  80.3 4.0 %collective-permute-start.9 = (bf16[1024,128]{1,0:T(8,128)(2,1)S(1)}, bf16[1024,128]{1,0:T(8,128)(2,1)S(1)}, u32[]{:S(2)}, u32[]{:S(2)}) collective-permute-start(bf16[1024,128]{1,0:T(8,128)(2,1)S(1)} %get-tuple-element.50), channel_id=1, source_target_pairs={{0,127},{1,2},{2,1},{3,4},{4,3},{5,6},{6,5},{7,8},{8,7},{9,10},{10... | collective-permute-start | bytes 786440 | tf_op jit(solution)/shard_map/ppermute | solution.py:343
  84.3 3.8 %collective-permute-done.8.got_e = bf16[1024,128]{1,0:T(8,128)(2,1)S(1)} collective-permute-done((bf16[1024,128]{1,0:T(8,128)(2,1)S(1)}, bf16[1024,128]{1,0:T(8,128)(2,1)S(1)}, u32[]{:S(2)}, u32[]{:S(2)}) %collective-permute-start.8) | collective-permute-done | bytes 262176 | tf_op jit(solution)/shard_map/ppermute | solution.py:347
  88.1 1.1 shard_map.73.base
  89.2 2.5 %collective-permute-done.9.got_o = bf16[1024,128]{1,0:T(8,128)(2,1)S(1)} collective-permute-done((bf16[1024,128]{1,0:T(8,128)(2,1)S(1)}, bf16[1024,128]{1,0:T(8,128)(2,1)S(1)}, u32[]{:S(2)}, u32[]{:S(2)}) %collective-permute-start.9) | collective-permute-done | bytes 262176 | tf_op jit(solution)/shard_map/ppermute | solution.py:343
  91.7 0.7 shard_map.74
  92.3 0.1 collective-permute-start.12
  92.4 0.1 collective-permute-start.11
  92.5 4.0 %collective-permute-start.10 = (f32[128,128]{1,0:T(8,128)S(1)}, f32[128,128]{1,0:T(8,128)S(1)}, u32[]{:S(2)}, u32[]{:S(2)}) collective-permute-start(f32[128,128]{1,0:T(8,128)S(1)} %get-tuple-element.51), channel_id=1, source_target_pairs={{0,1},{1,0},{2,3},{3,2},{4,5},{5,4},{6,7},{7,6},{8,9},{9,8},{10,11... | collective-permute-start | bytes 196616 | tf_op jit(solution)/shard_map/ppermute | solution.py:359
  96.5 2.1 %collective-permute-done.12 = f32[128,128]{1,0:T(8,128)S(1)} collective-permute-done((f32[128,128]{1,0:T(8,128)S(1)}, f32[128,128]{1,0:T(8,128)S(1)}, u32[]{:S(2)}, u32[]{:S(2)}) %collective-permute-start.12) | collective-permute-done | bytes 65568 | tf_op jit(solution)/shard_map/ppermute | solution.py:359
  98.6 0.0 collective-permute-done.11
  98.6 0.9 collective-permute-done.10
  99.5 0.1 collective-permute-start.15
  99.5 0.1 collective-permute-start.14
  99.6 4.0 %collective-permute-start.13 = (f32[128,128]{1,0:T(8,128)S(1)}, f32[128,128]{1,0:T(8,128)S(1)}, u32[]{:S(2)}, u32[]{:S(2)}) collective-permute-start(f32[128,128]{1,0:T(8,128)S(1)} %add_add_fusion.2), channel_id=1, source_target_pairs={{0,4},{1,5},{2,6},{3,7},{4,0},{5,1},{6,2},{7,3},{8,12},{9,13},{10,... | collective-permute-start | bytes 196616 | tf_op jit(solution)/shard_map/ppermute | solution.py:359
  103.6 2.1 %collective-permute-done.15 = f32[128,128]{1,0:T(8,128)S(1)} collective-permute-done((f32[128,128]{1,0:T(8,128)S(1)}, f32[128,128]{1,0:T(8,128)S(1)}, u32[]{:S(2)}, u32[]{:S(2)}) %collective-permute-start.15) | collective-permute-done | bytes 65568 | tf_op jit(solution)/shard_map/ppermute | solution.py:359
  105.7 0.0 collective-permute-done.14
  105.7 0.9 collective-permute-done.13
  106.6 0.1 collective-permute-start.16
  106.7 1.2 %collective-permute-done.16 = f32[128,128]{1,0:T(8,128)S(1)} collective-permute-done((f32[128,128]{1,0:T(8,128)S(1)}, f32[128,128]{1,0:T(8,128)S(1)}, u32[]{:S(2)}, u32[]{:S(2)}) %collective-permute-start.16) | collective-permute-done | bytes 65568 | tf_op jit(solution)/shard_map/ppermute | solution.py:359
  107.9 1.4 %collective-permute-start.19 = (f32[128,128]{1,0:T(8,128)S(1)}, f32[128,128]{1,0:T(8,128)S(1)}, u32[]{:S(2)}, u32[]{:S(2)}) collective-permute-start(f32[128,128]{1,0:T(8,128)S(1)} %add.36), channel_id=1, source_target_pairs={{0,96},{1,97},{2,98},{3,99},{4,100},{5,101},{6,102},{7,103},{8,104... | collective-permute-start | bytes 196616 | tf_op jit(solution)/shard_map/ppermute | solution.py:359
  109.4 0.0 collective-permute-start.18
  109.4 2.7 %collective-permute-start.17 = (f32[128,128]{1,0:T(8,128)S(1)}, f32[128,128]{1,0:T(8,128)S(1)}, u32[]{:S(2)}, u32[]{:S(2)}) collective-permute-start(f32[128,128]{1,0:T(8,128)S(1)} %add.36), channel_id=1, source_target_pairs={{0,32},{1,33},{2,34},{3,35},{4,36},{5,37},{6,38},{7,39},{8,40},{9,... | collective-permute-start | bytes 196616 | tf_op jit(solution)/shard_map/ppermute | solution.py:359
  112.1 2.1 %collective-permute-done.19 = f32[128,128]{1,0:T(8,128)S(1)} collective-permute-done((f32[128,128]{1,0:T(8,128)S(1)}, f32[128,128]{1,0:T(8,128)S(1)}, u32[]{:S(2)}, u32[]{:S(2)}) %collective-permute-start.19) | collective-permute-done | bytes 65568 | tf_op jit(solution)/shard_map/ppermute | solution.py:359
  114.2 1.3 %collective-permute-done.18 = f32[128,128]{1,0:T(8,128)S(1)} collective-permute-done((f32[128,128]{1,0:T(8,128)S(1)}, f32[128,128]{1,0:T(8,128)S(1)}, u32[]{:S(2)}, u32[]{:S(2)}) %collective-permute-start.18) | collective-permute-done | bytes 65568 | tf_op jit(solution)/shard_map/ppermute | solution.py:359
  115.5 0.0 collective-permute-done.17
  115.5 4.3 %shard_map.75 = f32[1024,128]{1,0:T(8,128)} custom-call(f32[128,128]{1,0:T(8,128)S(1)} %add_add_fusion.gram, bf16[1024,128]{1,0:T(8,128)(2,1)S(1)} %get-tuple-element.52.y), custom_call_target="tpu_custom_call" | custom-call | flops 536870912 | bytes 1000000 | tf_op jit(solution)/shard_map/pallas_call | solution.py:432
  (7 shorter events, 0.1 us)
Async XLA Ops:
  0.0 14.9 %copy-start.2 = (bf16[1024,128]{1,0:T(8,128)(2,1)S(1)}, bf16[1024,128]{1,0:T(8,128)(2,1)}, u32[]{:S(2)}) copy-start(bf16[1024,128]{1,0:T(8,128)(2,1)} %older.1) | copy-start | bytes 786436
  0.0 14.7 %copy-start.6 = (f32[1024]{0:T(1024)S(1)}, f32[1024]{0:T(1024)}, u32[]{:S(2)}) copy-start(f32[1024]{0:T(1024)} %param.10) | copy-start | bytes 12292
  5.3 19.5 %collective-permute-start = (bf16[3072,128]{1,0:T(8,128)(2,1)}, bf16[3072,128]{1,0:T(8,128)(2,1)S(1)}, u32[]{:S(2)}, u32[]{:S(2)}) collective-permute-start(bf16[3072,128]{1,0:T(8,128)(2,1)} %get-tuple-element.35.to_e), channel_id=1, source_target_pairs={{0,1},{1,0},{2,3},{3,2},{4,5},{5,4},{6,7},{7,6},{8,9},{9,8},{10,11... | collective-permute-start | bytes 2359304 | tf_op jit(solution)/shard_map/ppermute | solution.py:347
  7.1 25.0 %collective-permute-start.1 = (bf16[3072,128]{1,0:T(8,128)(2,1)}, bf16[3072,128]{1,0:T(8,128)(2,1)S(1)}, u32[]{:S(2)}, u32[]{:S(2)}) collective-permute-start(bf16[3072,128]{1,0:T(8,128)(2,1)} %get-tuple-element.36.to_o), channel_id=1, source_target_pairs={{0,127},{1,2},{2,1},{3,4},{4,3},{5,6},{6,5},{7,8},{8,7},{9,10},{10... | collective-permute-start | bytes 2359304 | tf_op jit(solution)/shard_map/ppermute | solution.py:343
  14.9 1.6 %copy-start = (bf16[1024,1024]{1,0:T(8,128)(2,1)S(1)}, bf16[1024,1024]{1,0:T(8,128)(2,1)}, u32[]{:S(2)}) copy-start(bf16[1024,1024]{1,0:T(8,128)(2,1)} %get-tuple-element.30.edge.edge_in) | copy-start | bytes 6291460
  16.5 1.6 %copy-start.3 = (bf16[1024,1024]{1,0:T(8,128)(2,1)S(1)}, bf16[1024,1024]{1,0:T(8,128)(2,1)}, u32[]{:S(2)}) copy-start(bf16[1024,1024]{1,0:T(8,128)(2,1)} %get-tuple-element.29.own) | copy-start | bytes 6291460
  18.1 14.1 %copy-start.1 = (bf16[1024,1024]{1,0:T(8,128)(2,1)S(1)}, bf16[1024,1024]{1,0:T(8,128)(2,1)}, u32[]{:S(2)}) copy-start(bf16[1024,1024]{1,0:T(8,128)(2,1)} %get-tuple-element.30.edge.edge_in) | copy-start | bytes 6291460
  18.1 14.1 %copy-start.4 = (bf16[3072,128]{1,0:T(8,128)(2,1)S(1)}, bf16[3072,128]{1,0:T(8,128)(2,1)}, u32[]{:S(2)}) copy-start(bf16[3072,128]{1,0:T(8,128)(2,1)} %get-tuple-element.35.to_e) | copy-start | bytes 2359300
  18.1 14.1 %copy-start.5 = (bf16[3072,128]{1,0:T(8,128)(2,1)S(1)}, bf16[3072,128]{1,0:T(8,128)(2,1)}, u32[]{:S(2)}) copy-start(bf16[3072,128]{1,0:T(8,128)(2,1)} %get-tuple-element.36.to_o) | copy-start | bytes 2359300
  34.5 7.4 %collective-permute-start.2 = (bf16[1024,128]{1,0:T(8,128)(2,1)S(1)}, bf16[1024,128]{1,0:T(8,128)(2,1)S(1)}, u32[]{:S(2)}, u32[]{:S(2)}) collective-permute-start(bf16[1024,128]{1,0:T(8,128)(2,1)S(1)} %get-tuple-element.39), channel_id=1, source_target_pairs={{0,1},{1,0},{2,3},{3,2},{4,5},{5,4},{6,7},{7,6},{8,9},{9,8},{10,11... | collective-permute-start | bytes 786440 | tf_op jit(solution)/shard_map/ppermute | solution.py:347
  34.6 13.5 %collective-permute-start.3 = (bf16[1024,128]{1,0:T(8,128)(2,1)S(1)}, bf16[1024,128]{1,0:T(8,128)(2,1)S(1)}, u32[]{:S(2)}, u32[]{:S(2)}) collective-permute-start(bf16[1024,128]{1,0:T(8,128)(2,1)S(1)} %get-tuple-element.41), channel_id=1, source_target_pairs={{0,127},{1,2},{2,1},{3,4},{4,3},{5,6},{6,5},{7,8},{8,7},{9,10},{10... | collective-permute-start | bytes 786440 | tf_op jit(solution)/shard_map/ppermute | solution.py:343
  49.1 6.5 %collective-permute-start.4 = (bf16[1024,128]{1,0:T(8,128)(2,1)S(1)}, bf16[1024,128]{1,0:T(8,128)(2,1)S(1)}, u32[]{:S(2)}, u32[]{:S(2)}) collective-permute-start(bf16[1024,128]{1,0:T(8,128)(2,1)S(1)} %get-tuple-element.43), channel_id=1, source_target_pairs={{0,1},{1,0},{2,3},{3,2},{4,5},{5,4},{6,7},{7,6},{8,9},{9,8},{10,11... | collective-permute-start | bytes 786440 | tf_op jit(solution)/shard_map/ppermute | solution.py:347
  49.2 14.0 %collective-permute-start.5 = (bf16[1024,128]{1,0:T(8,128)(2,1)S(1)}, bf16[1024,128]{1,0:T(8,128)(2,1)S(1)}, u32[]{:S(2)}, u32[]{:S(2)}) collective-permute-start(bf16[1024,128]{1,0:T(8,128)(2,1)S(1)} %get-tuple-element.44), channel_id=1, source_target_pairs={{0,127},{1,2},{2,1},{3,4},{4,3},{5,6},{6,5},{7,8},{8,7},{9,10},{10... | collective-permute-start | bytes 786440 | tf_op jit(solution)/shard_map/ppermute | solution.py:343
  64.2 6.5 %collective-permute-start.6 = (bf16[1024,128]{1,0:T(8,128)(2,1)S(1)}, bf16[1024,128]{1,0:T(8,128)(2,1)S(1)}, u32[]{:S(2)}, u32[]{:S(2)}) collective-permute-start(bf16[1024,128]{1,0:T(8,128)(2,1)S(1)} %get-tuple-element.46), channel_id=1, source_target_pairs={{0,1},{1,0},{2,3},{3,2},{4,5},{5,4},{6,7},{7,6},{8,9},{9,8},{10,11... | collective-permute-start | bytes 786440 | tf_op jit(solution)/shard_map/ppermute | solution.py:347
  64.3 14.7 %collective-permute-start.7 = (bf16[1024,128]{1,0:T(8,128)(2,1)S(1)}, bf16[1024,128]{1,0:T(8,128)(2,1)S(1)}, u32[]{:S(2)}, u32[]{:S(2)}) collective-permute-start(bf16[1024,128]{1,0:T(8,128)(2,1)S(1)} %get-tuple-element.47), channel_id=1, source_target_pairs={{0,127},{1,2},{2,1},{3,4},{4,3},{5,6},{6,5},{7,8},{8,7},{9,10},{10... | collective-permute-start | bytes 786440 | tf_op jit(solution)/shard_map/ppermute | solution.py:343
  80.3 7.9 %collective-permute-start.8 = (bf16[1024,128]{1,0:T(8,128)(2,1)S(1)}, bf16[1024,128]{1,0:T(8,128)(2,1)S(1)}, u32[]{:S(2)}, u32[]{:S(2)}) collective-permute-start(bf16[1024,128]{1,0:T(8,128)(2,1)S(1)} %get-tuple-element.49), channel_id=1, source_target_pairs={{0,1},{1,0},{2,3},{3,2},{4,5},{5,4},{6,7},{7,6},{8,9},{9,8},{10,11... | collective-permute-start | bytes 786440 | tf_op jit(solution)/shard_map/ppermute | solution.py:347
  80.3 11.3 %collective-permute-start.9 = (bf16[1024,128]{1,0:T(8,128)(2,1)S(1)}, bf16[1024,128]{1,0:T(8,128)(2,1)S(1)}, u32[]{:S(2)}, u32[]{:S(2)}) collective-permute-start(bf16[1024,128]{1,0:T(8,128)(2,1)S(1)} %get-tuple-element.50), channel_id=1, source_target_pairs={{0,127},{1,2},{2,1},{3,4},{4,3},{5,6},{6,5},{7,8},{8,7},{9,10},{10... | collective-permute-start | bytes 786440 | tf_op jit(solution)/shard_map/ppermute | solution.py:343
  92.3 6.3 %collective-permute-start.12 = (f32[128,128]{1,0:T(8,128)S(1)}, f32[128,128]{1,0:T(8,128)S(1)}, u32[]{:S(2)}, u32[]{:S(2)}) collective-permute-start(f32[128,128]{1,0:T(8,128)S(1)} %get-tuple-element.51), channel_id=1, source_target_pairs={{0,3},{1,2},{2,1},{3,0},{4,7},{5,6},{6,5},{7,4},{8,11},{9,10},{10,... | collective-permute-start | bytes 196616 | tf_op jit(solution)/shard_map/ppermute | solution.py:359
  92.4 6.2 %collective-permute-start.11 = (f32[128,128]{1,0:T(8,128)S(1)}, f32[128,128]{1,0:T(8,128)S(1)}, u32[]{:S(2)}, u32[]{:S(2)}) collective-permute-start(f32[128,128]{1,0:T(8,128)S(1)} %get-tuple-element.51), channel_id=1, source_target_pairs={{0,2},{1,3},{2,0},{3,1},{4,6},{5,7},{6,4},{7,5},{8,10},{9,11},{10,... | collective-permute-start | bytes 196616 | tf_op jit(solution)/shard_map/ppermute | solution.py:359
  92.5 6.9 %collective-permute-start.10 = (f32[128,128]{1,0:T(8,128)S(1)}, f32[128,128]{1,0:T(8,128)S(1)}, u32[]{:S(2)}, u32[]{:S(2)}) collective-permute-start(f32[128,128]{1,0:T(8,128)S(1)} %get-tuple-element.51), channel_id=1, source_target_pairs={{0,1},{1,0},{2,3},{3,2},{4,5},{5,4},{6,7},{7,6},{8,9},{9,8},{10,11... | collective-permute-start | bytes 196616 | tf_op jit(solution)/shard_map/ppermute | solution.py:359
  99.5 6.3 %collective-permute-start.15 = (f32[128,128]{1,0:T(8,128)S(1)}, f32[128,128]{1,0:T(8,128)S(1)}, u32[]{:S(2)}, u32[]{:S(2)}) collective-permute-start(f32[128,128]{1,0:T(8,128)S(1)} %add_add_fusion.2), channel_id=1, source_target_pairs={{0,12},{1,13},{2,14},{3,15},{4,8},{5,9},{6,10},{7,11},{8,4},{9,5},... | collective-permute-start | bytes 196616 | tf_op jit(solution)/shard_map/ppermute | solution.py:359
  99.5 6.2 %collective-permute-start.14 = (f32[128,128]{1,0:T(8,128)S(1)}, f32[128,128]{1,0:T(8,128)S(1)}, u32[]{:S(2)}, u32[]{:S(2)}) collective-permute-start(f32[128,128]{1,0:T(8,128)S(1)} %add_add_fusion.2), channel_id=1, source_target_pairs={{0,8},{1,9},{2,10},{3,11},{4,12},{5,13},{6,14},{7,15},{8,0},{9,1},... | collective-permute-start | bytes 196616 | tf_op jit(solution)/shard_map/ppermute | solution.py:359
  99.6 6.9 %collective-permute-start.13 = (f32[128,128]{1,0:T(8,128)S(1)}, f32[128,128]{1,0:T(8,128)S(1)}, u32[]{:S(2)}, u32[]{:S(2)}) collective-permute-start(f32[128,128]{1,0:T(8,128)S(1)} %add_add_fusion.2), channel_id=1, source_target_pairs={{0,4},{1,5},{2,6},{3,7},{4,0},{5,1},{6,2},{7,3},{8,12},{9,13},{10,... | collective-permute-start | bytes 196616 | tf_op jit(solution)/shard_map/ppermute | solution.py:359
  106.6 1.3 %collective-permute-start.16 = (f32[128,128]{1,0:T(8,128)S(1)}, f32[128,128]{1,0:T(8,128)S(1)}, u32[]{:S(2)}, u32[]{:S(2)}) collective-permute-start(f32[128,128]{1,0:T(8,128)S(1)} %add_add_fusion.1), channel_id=1, source_target_pairs={{0,16},{1,17},{2,18},{3,19},{4,20},{5,21},{6,22},{7,23},{8,24},{9,... | collective-permute-start | bytes 196616 | tf_op jit(solution)/shard_map/ppermute | solution.py:359
  107.9 6.3 %collective-permute-start.19 = (f32[128,128]{1,0:T(8,128)S(1)}, f32[128,128]{1,0:T(8,128)S(1)}, u32[]{:S(2)}, u32[]{:S(2)}) collective-permute-start(f32[128,128]{1,0:T(8,128)S(1)} %add.36), channel_id=1, source_target_pairs={{0,96},{1,97},{2,98},{3,99},{4,100},{5,101},{6,102},{7,103},{8,104... | collective-permute-start | bytes 196616 | tf_op jit(solution)/shard_map/ppermute | solution.py:359
  109.4 6.1 %collective-permute-start.18 = (f32[128,128]{1,0:T(8,128)S(1)}, f32[128,128]{1,0:T(8,128)S(1)}, u32[]{:S(2)}, u32[]{:S(2)}) collective-permute-start(f32[128,128]{1,0:T(8,128)S(1)} %add.36), channel_id=1, source_target_pairs={{0,64},{1,65},{2,66},{3,67},{4,68},{5,69},{6,70},{7,71},{8,72},{9,... | collective-permute-start | bytes 196616 | tf_op jit(solution)/shard_map/ppermute | solution.py:359
  109.4 6.1 %collective-permute-start.17 = (f32[128,128]{1,0:T(8,128)S(1)}, f32[128,128]{1,0:T(8,128)S(1)}, u32[]{:S(2)}, u32[]{:S(2)}) collective-permute-start(f32[128,128]{1,0:T(8,128)S(1)} %add.36), channel_id=1, source_target_pairs={{0,32},{1,33},{2,34},{3,35},{4,36},{5,37},{6,38},{7,39},{8,40},{9,... | collective-permute-start | bytes 196616 | tf_op jit(solution)/shard_map/ppermute | solution.py:359

commit v2 on v1

--- a/solution.py
+++ b/solution.py
@@ -182,32 +182,57 @@
             body(even)
 
 
-def from_right(a, edge, got, halo=0, terms=2 * B):
+def halo_right(a, edge, got, halo=0):
     wide = 1 if a == 0 else 2
-    total = dot(edge[rows(a), rows(0, wide)], got[pl.ds(halo, wide * B), :])
-    if a >= 2:
-        total += got[pl.ds(terms + (a - 2) * B, B), :].astype(F32)
-    return total
-
-
-def from_left(a, edge, got, halo=0, terms=2 * B):
+    return dot(edge[rows(a), rows(0, wide)], got[pl.ds(halo, wide * B), :])
+
+
+def halo_left(a, edge, got, halo=0):
     skip = 1 if a == ROWS - 1 else 0
-    total = dot(edge[rows(a), rows(2 + skip, 2 - skip)], got[pl.ds(halo + skip * B, (2 - skip) * B), :])
-    if a < 2:
-        total += got[pl.ds(terms + a * B, B), :].astype(F32)
-    return total
-
-
-def send_parts(edge_t, y, send_right, send_left):
-    send_right[pl.ds(0, 2 * B), :] = y[pl.ds(2 * B, 2 * B), :]
-    send_left[pl.ds(0, 2 * B), :] = y[pl.ds(0, 2 * B), :]
-    send_right[pl.ds(2 * B, B), :] = dot(edge_t[rows(0), :], y[...]).astype(BF16)
-    send_right[pl.ds(3 * B, B), :] = dot(edge_t[rows(1), rows(1, 3)], y[rows(1, 3), :]).astype(BF16)
-    send_left[pl.ds(2 * B, B), :] = dot(edge_t[rows(2), rows(0, 3)], y[rows(0, 3), :]).astype(BF16)
-    send_left[pl.ds(3 * B, B), :] = dot(edge_t[rows(3), :], y[...]).astype(BF16)
-
-
-def first_post_kernel(base, edge_in, edge_t_in, to_e, to_o, got_e, got_o, edge, edge_t, y, send_e, send_o):
+    return dot(edge[rows(a), rows(2 + skip, 2 - skip)], got[pl.ds(halo + skip * B, (2 - skip) * B), :])
+
+
+def terms_of(a, got_left, got_right, start=0):
+    got = got_left if a < 2 else got_right
+    return got[pl.ds(start + (a % 2) * B, B), :].astype(F32)
+
+
+HALF = K // 2
+
+
+def half_mask(half):
+    lane = lax.broadcasted_iota(jnp.int32, (B, K), 1)
+    return (lane < HALF) if half == 0 else (lane >= HALF)
+
+
+def take(sides, got_e, got_o):
+    parity = lax.rem(lax.axis_index(AXES), 2)
+    sides[parity] = got_e[...]
+    sides[1 - parity] = got_o[...]
+
+
+def give(sides, send_e, send_o):
+    parity = lax.rem(lax.axis_index(AXES), 2)
+    send_e[...] = sides[parity]
+    send_o[...] = sides[1 - parity]
+
+
+def pack(half, edge_t, y, sides, spare):
+    mine = half_mask(half)
+    for a in range(ROWS):
+        value = jnp.where(mine, y[rows(a), :].astype(F32), 0.0)
+        spare[rows(a), :] = pltpu.roll(value, HALF, 1).astype(BF16)
+
+    def put(side, i, row, terms):
+        sides[side, rows(i), :] = jnp.where(mine, y[rows(row), :].astype(F32), terms).astype(BF16)
+
+    put(0, 0, 2, dot(edge_t[rows(0), :], spare[...]))
+    put(0, 1, 3, dot(edge_t[rows(1), rows(1, 3)], spare[rows(1, 3), :]))
+    put(1, 0, 0, dot(edge_t[rows(2), rows(0, 3)], spare[rows(0, 3), :]))
+    put(1, 1, 1, dot(edge_t[rows(3), :], spare[...]))
+
+
+def first_post_kernel(base, edge_in, edge_t_in, to_e, to_o, got_e, got_o, edge, edge_t, y, send_e, send_o, send_e2, send_o2, spare, sides):
     edge[...] = edge_in[...]
     edge_t[...] = edge_t_in[...]
 
@@ -225,43 +250,44 @@
             edge[rows(r), rows(c)] = (edge[rows(r), rows(c)].astype(F32) + block.T).astype(BF16)
         halo = HANDED + 2 * B
         for a in range(ROWS):
-            total = base[rows(a), :] + from_right(a, edge, got_right, halo, HANDED)
-            total += from_left(a, edge, got_left, halo + 2 * B, HANDED)
+            total = base[rows(a), :] + halo_right(a, edge, got_right, halo)
+            total += halo_left(a, edge, got_left, halo + 2 * B) + terms_of(a, got_left, got_right, HANDED)
             for places, source, got, start in ((TO_LEFT, to_left, got_left, 0), (TO_RIGHT, to_right, got_right, 8)):
                 for i, (row, p) in enumerate(places):
                     if row == a:
                         total += dot(read_block(source, i), got[pl.ds(halo + (p - start) * B, B), :])
             y[rows(a), :] = (0.5 * total).astype(BF16)
-        send_parts(edge_t, y, *((send_e, send_o) if even else (send_o, send_e)))
-
     by_parity(body)
-
-
-def local_kernel(sym, diag, y, older, edge, got_e, base):
+    for half, to_e, to_o in ((0, send_e, send_o), (1, send_e2, send_o2)):
+        pack(half, edge_t, y, sides, spare)
+        give(sides, to_e, to_o)
+
+
+def local_kernel(sym, diag, y, older, base):
     base[...] = diag[...] * y[...].astype(F32) - older[...].astype(F32) + dot(sym[...], y[...])
 
-    def body(even):
-        for a in range(ROWS):
-            base[rows(a), :] += (from_right if even else from_left)(a, edge, got_e)
-
-    by_parity(body)
-
-
-def receive(even, base, edge, got_o, y):
-    for a in range(ROWS):
-        y[rows(a), :] = (base[rows(a), :] + (from_left if even else from_right)(a, edge, got_o)).astype(BF16)
-
-
-def post_kernel(base, edge, edge_t, got_o, y, send_e, send_o):
-    def body(even):
-        receive(even, base, edge, got_o, y)
-        send_parts(edge_t, y, *((send_e, send_o) if even else (send_o, send_e)))
-
-    by_parity(body)
-
-
-def last_kernel(base, edge, got_o, y, gram):
-    by_parity(lambda even: receive(even, base, edge, got_o, y))
+
+def receive(half, base, edge, got_e, got_o, y_in, y, sides):
+    take(sides, got_e, got_o)
+    right, left = sides.at[0], sides.at[1]
+    for a in range(ROWS):
+        total = base[rows(a), :] + halo_right(a, edge, right) + halo_left(a, edge, left)
+        total += pltpu.roll(terms_of(a, left, right), HALF, 1)
+        y[rows(a), :] = jnp.where(half_mask(half), total, y_in[rows(a), :].astype(F32)).astype(BF16)
+
+
+def post_kernel(half, base, edge, edge_t, got_e, got_o, y_in, y, send_e, send_o, spare, sides):
+    receive(half, base, edge, got_e, got_o, y_in, y, sides)
+    pack(half, edge_t, y, sides, spare)
+    give(sides, send_e, send_o)
+
+
+def last_first_kernel(base, edge, got_e, got_o, y_in, y, sides):
+    receive(0, base, edge, got_e, got_o, y_in, y, sides)
+
+
+def last_kernel(base, edge, got_e, got_o, y_in, y, gram, sides):
+    receive(1, base, edge, got_e, got_o, y_in, y, sides)
     gram[...] = lax.dot_general(y[...], y[...], (((0,), (0,)), ((), ())), preferred_element_type=F32)
 
 
@@ -347,6 +373,11 @@
     return lax.ppermute(value, AXES, [(i, i ^ 1) for i in range(lax.axis_size(AXES))])
 
 
+def exchange(send_e, send_o):
+    got_o = swap_o(send_o)
+    return swap_e(send_e), got_o
+
+
 def group_sum(value, stride, size):
     count = lax.axis_size(AXES)
     parts = [value]
@@ -412,20 +443,32 @@
     diag, sym, edge_t, base = call(first_local_kernel, [column, square, square, tall32], [VMEM] * 4, product, 10_000_000)(
         own, edge, onsite[:, None], y0
     )
-    edge, edge_t, y, send_e, send_o = call(
-        first_post_kernel, [square, square, tall, tall, tall], [VMEM] * 7, 2 * product, 9_000_000, (), {1: 0, 2: 1}
+    part = ((2 * B, K), BF16)
+    sides = pltpu.VMEM((2, 2 * B, K), BF16)
+    spare = [pltpu.VMEM((OWN, K), BF16), sides]
+    edge, edge_t, y, *sends = call(
+        first_post_kernel, [square, square, tall, part, part, part, part], [VMEM] * 7, 3 * product, 9_000_000, spare, {1: 0, 2: 1}
     )(base, edge, edge_t, to_e, to_o, got_e, got_o)
     older = y0
+    got = exchange(*sends[:2])
+    got2 = exchange(*sends[2:])
     for step in range(1, DEG):
-        got_o, got_e = swap_o(send_o), swap_e(send_e)
-        base = call(local_kernel, [tall32], [VMEM] * 6, product, 3_500_000)(sym, diag, y, older, edge, got_e)[0]
+        base = call(local_kernel, [tall32], [VMEM] * 4, product, 3_500_000)(sym, diag, y, older)[0]
         older = y
         if step < DEG - 1:
-            y, send_e, send_o = call(post_kernel, [tall, tall, tall], [VMEM] * 4, 2 * product, 6_000_000)(
-                base, edge, edge_t, got_o
+            outs = [tall, part, part]
+            specs = [VMEM] * 6
+            y, *sends = call(functools.partial(post_kernel, 0), outs, specs, 2 * product, 6_000_000, spare)(
+                base, edge, edge_t, *got, y
             )
+            got = exchange(*sends)
+            y, *sends = call(functools.partial(post_kernel, 1), outs, specs, 2 * product, 6_000_000, spare)(
+                base, edge, edge_t, *got2, y
+            )
+            got2 = exchange(*sends)
         else:
-            y, gram = call(last_kernel, [tall, ((K, K), F32)], [VMEM] * 3, product, 4_000_000)(base, edge, got_o)
+            y = call(last_first_kernel, [tall], [VMEM] * 5, product, 4_000_000, [sides])(base, edge, *got, y)[0]
+            y, gram = call(last_kernel, [tall, ((K, K), F32)], [VMEM] * 5, product, 4_000_000, [sides])(base, edge, *got2, y)
     for stride, size in digits():
         gram = group_sum(gram, stride, size)
     scale = float(np.sqrt(total * B))

time: 120 us -> 119 us (level)
  waiting for transfers between devices: 49.9 us -> 33.5 us
  starting transfers between devices: 44.4 us -> 54.4 us
  Pallas kernels: 21.7 us -> 26.8 us
    ppermute x5 -> x9, waiting for transfers between devices: 28.8 us -> 14.2 us  [swap_o(): lax.ppermute(value, AXES, [(i, (i + 1 if i % 2 else i - 1) % count) for i...]
    ppermute x5 -> x9, starting transfers between devices: 29.7 us -> 39.4 us  [swap_o(): lax.ppermute(value, AXES, [(i, (i + 1 if i % 2 else i - 1) % count) for i...]
    pallas_call x9 -> x13, Pallas kernels: 10.6 us -> 15.5 us  [the longest x3 4.07 us: local(): call(functools.partial(post_kernel, 1), outs, specs, 2 * product, 6000000...]
    ppermute x5 -> x9, waiting for transfers between devices: 10.7 us -> 8.94 us  [swap_e(): lax.ppermute(value, AXES, [(i, i ^ 1) for i in range(lax.axis_size(AXES))])]
    ppermute x5 -> x9, starting transfers between devices: 2.2 us -> 2.45 us  [swap_e(): lax.ppermute(value, AXES, [(i, i ^ 1) for i in range(lax.axis_size(AXES))])]
  transfers between devices with their start and end apart: 20 -> 28, of which waited for: 17 -> 13; matrix products, arithmetic and copies ran while one was open for 0% -> 0% of each run, Pallas kernels for 5% -> 11%
where the time goes in v2:
time: 119 us; the launch traced here: 118 us
  starting transfers between devices  54.4 us (46%)
  waiting for transfers between devices  33.5 us (28%)
  Pallas kernels  26.8 us (23%)
  local copies, waits for them, and re-layouts  3.41 us (3%)
    ppermute x9, starting transfers between devices, swap_o(): lax.ppermute(value, AXES, [(i, (i + 1 if i % 2 else i - 1) % count) for i...  39.4 us
    ppermute x9, waiting for transfers between devices, swap_o(): lax.ppermute(value, AXES, [(i, (i + 1 if i % 2 else i - 1) % count) for i...  14.2 us
    ppermute x10, starting transfers between devices, group_sum(): parts.append(lax.ppermute(value, AXES, pairs))  12.6 us
    ppermute x10, waiting for transfers between devices, group_sum(): parts.append(lax.ppermute(value, AXES, pairs))  10.4 us
    ppermute x9, waiting for transfers between devices, swap_e(): lax.ppermute(value, AXES, [(i, i ^ 1) for i in range(lax.axis_size(AXES))])  8.94 us
    pallas_call x1, Pallas kernels, local(): call(functools.partial(prep_kernel, total), [square, square, message, mes...  5.43 us
    pallas_call x1, Pallas kernels, local(): call(functools.partial(finish_kernel, scale), [tall32], [VMEM] * 2, 2 * p...  4.27 us
    pallas_call x3, Pallas kernels, local(): call(functools.partial(post_kernel, 1), outs, specs, 2 * product, 6000000...  4.07 us
  transfers between devices with their start and end apart: 28, of which 13 were waited for; matrix products, arithmetic and copies ran while one was open for 0% of the time, Pallas kernels for 11%

profile of v2, /device:TPU:0, one launch (start us, length us, event | category | flops | bytes accessed | tf_op | source)
XLA Modules:
  0.0 118.4 jit_solution(11804690487118788979)
XLA Ops:
  0.0 5.4 %shard_map.64 = (bf16[1024,1024]{1,0:T(8,128)(2,1)}, bf16[1024,1024]{1,0:T(8,128)(2,1)}, bf16[3072,128]{1,0:T(8,128)(2,1)}, bf16[3072,128]{1,0:T(8,128)(2,1)}) custom-call(f32[4,10]{1,0:T(4,128)} %scales_in.1, s32[4,10]{1,0:T(4,128)} %columns_in.1, s32[4]{0:T(128)} %live_in.1, bf16[4,10,256,256]{3,2,1,0:T(8,128)(2,1)} %blocks.1, bf16[1024,128]{1,0:T(8,128)(2,1)} %older.1), custom_call_target="tpu_custom_call" | custom-call | flops 268435456 | bytes 10000000 | tf_op jit(solution)/shard_map/pallas_call | solution.py:418
  5.4 1.6 %collective-permute-start = (bf16[3072,128]{1,0:T(8,128)(2,1)}, bf16[3072,128]{1,0:T(8,128)(2,1)S(1)}, u32[]{:S(2)}, u32[]{:S(2)}) collective-permute-start(bf16[3072,128]{1,0:T(8,128)(2,1)} %get-tuple-element.46.to_e), channel_id=1, source_target_pairs={{0,1},{1,0},{2,3},{3,2},{4,5},{5,4},{6,7},{7,6},{8,9},{9,8},{10,11... | collective-permute-start | bytes 2359304 | tf_op jit(solution)/shard_map/ppermute | solution.py:373
  7.1 7.1 %collective-permute-start.1 = (bf16[3072,128]{1,0:T(8,128)(2,1)}, bf16[3072,128]{1,0:T(8,128)(2,1)S(1)}, u32[]{:S(2)}, u32[]{:S(2)}) collective-permute-start(bf16[3072,128]{1,0:T(8,128)(2,1)} %get-tuple-element.47.to_o), channel_id=1, source_target_pairs={{0,127},{1,2},{2,1},{3,4},{4,3},{5,6},{6,5},{7,8},{8,7},{9,10},{10... | collective-permute-start | bytes 2359304 | tf_op jit(solution)/shard_map/ppermute | solution.py:369
  14.2 0.2 copy.9.onsite
  14.5 1.6 %copy-done = bf16[1024,1024]{1,0:T(8,128)(2,1)S(1)} copy-done((bf16[1024,1024]{1,0:T(8,128)(2,1)S(1)}, bf16[1024,1024]{1,0:T(8,128)(2,1)}, u32[]{:S(2)}) %copy-start) | copy-done | bytes 2097176
  16.0 1.6 %copy-done.3 = bf16[1024,1024]{1,0:T(8,128)(2,1)S(1)} copy-done((bf16[1024,1024]{1,0:T(8,128)(2,1)S(1)}, bf16[1024,1024]{1,0:T(8,128)(2,1)}, u32[]{:S(2)}) %copy-start.3) | copy-done | bytes 2097176
  17.6 1.6 %shard_map.65 = (f32[1024,1]{1,0:T(8,128)S(1)}, bf16[1024,1024]{1,0:T(8,128)(2,1)S(1)}, bf16[1024,1024]{1,0:T(8,128)(2,1)S(1)}, f32[1024,128]{1,0:T(8,128)S(1)}) custom-call(bf16[1024,1024]{1,0:T(8,128)(2,1)S(1)} %copy-done.3, bf16[1024,1024]{1,0:T(8,128)(2,1)S(1)} %copy-done, f32[1024,1]{1,0:T(8,128)S(1)} %copy.9.onsite, bf16[1024,128]{1,0:T(8,128)(2,1)S(1)} %copy-done.2), custom_call_target="tpu_custom_call" | custom-call | flops 268435456 | bytes 10000000 | tf_op jit(solution)/shard_map/pallas_call | solution.py:443
  19.3 5.5 %collective-permute-done.got_e = bf16[3072,128]{1,0:T(8,128)(2,1)S(1)} collective-permute-done((bf16[3072,128]{1,0:T(8,128)(2,1)}, bf16[3072,128]{1,0:T(8,128)(2,1)S(1)}, u32[]{:S(2)}, u32[]{:S(2)}) %collective-permute-start) | collective-permute-done | bytes 786464 | tf_op jit(solution)/shard_map/ppermute | solution.py:373
  24.8 6.9 %collective-permute-done.1.got_o = bf16[3072,128]{1,0:T(8,128)(2,1)S(1)} collective-permute-done((bf16[3072,128]{1,0:T(8,128)(2,1)}, bf16[3072,128]{1,0:T(8,128)(2,1)S(1)}, u32[]{:S(2)}, u32[]{:S(2)}) %collective-permute-start.1) | collective-permute-done | bytes 786464 | tf_op jit(solution)/shard_map/ppermute | solution.py:369
  31.7 2.9 %shard_map.66 = (bf16[1024,1024]{1,0:T(8,128)(2,1)S(1)}, bf16[1024,1024]{1,0:T(8,128)(2,1)S(1)}, bf16[1024,128]{1,0:T(8,128)(2,1)S(1)}, bf16[512,128]{1,0:T(8,12...) custom-call(f32[1024,128]{1,0:T(8,128)S(1)} %get-tuple-element.44.ba, ...), custom_call_target="tpu_custom_call", output_to_operand_aliasing={{0}: (1, {}), {1}: (2, {})} | custom-call | flops 805306368 | bytes 9000000 | tf_op jit(solution)/shard_map/pallas_call | solution.py:449
  34.6 0.1 collective-permute-start.4
  34.7 7.0 %collective-permute-start.5 = (bf16[512,128]{1,0:T(8,128)(2,1)S(1)}, bf16[512,128]{1,0:T(8,128)(2,1)S(1)}, u32[]{:S(2)}, u32[]{:S(2)}) collective-permute-start(bf16[512,128]{1,0:T(8,128)(2,1)S(1)} %get-tuple-element.54), channel_id=1, source_target_pairs={{0,127},{1,2},{2,1},{3,4},{4,3},{5,6},{6,5},{7,8},{8,7},{9,10},{10... | collective-permute-start | bytes 393224 | tf_op jit(solution)/shard_map/ppermute | solution.py:369
  41.7 1.4 %collective-permute-start.3 = (bf16[512,128]{1,0:T(8,128)(2,1)S(1)}, bf16[512,128]{1,0:T(8,128)(2,1)S(1)}, u32[]{:S(2)}, u32[]{:S(2)}) collective-permute-start(bf16[512,128]{1,0:T(8,128)(2,1)S(1)} %get-tuple-element.52), channel_id=1, source_target_pairs={{0,127},{1,2},{2,1},{3,4},{4,3},{5,6},{6,5},{7,8},{8,7},{9,10},{10... | collective-permute-start | bytes 393224 | tf_op jit(solution)/shard_map/ppermute | solution.py:369
  43.1 0.7 shard_map.67.base
  43.8 0.0 collective-permute-done.4.got_e
  43.8 2.0 %collective-permute-done.5.got_o = bf16[512,128]{1,0:T(8,128)(2,1)S(1)} collective-permute-done((bf16[512,128]{1,0:T(8,128)(2,1)S(1)}, bf16[512,128]{1,0:T(8,128)(2,1)S(1)}, u32[]{:S(2)}, u32[]{:S(2)}) %collective-permute-start.5) | collective-permute-done | bytes 131104 | tf_op jit(solution)/shard_map/ppermute | solution.py:369
  45.8 1.4 %shard_map.68 = (bf16[1024,128]{1,0:T(8,128)(2,1)S(1)}, bf16[512,128]{1,0:T(8,128)(2,1)S(1)}, bf16[512,128]{1,0:T(8,128)(2,1)S(1)}) custom-call(f32[1024,128]{1,0:T(8,128)S(1)} %shard_map.67.base, bf16[1024,1024]{1,0:T(8,128)(2,1)S(1)} %get-tuple-element.49.edge, bf16[1024,1024]{1,0:T(8,128)(2,1)S(1)} %get-tuple-element.50.edge_t, ...), custom_call_target="tpu_custom_call" | custom-call | flops 536870912 | bytes 6000000 | tf_op jit(solution)/shard_map/pallas_call | solution.py:461
  47.1 0.1 collective-permute-start.8
  47.2 6.5 %collective-permute-start.9 = (bf16[512,128]{1,0:T(8,128)(2,1)S(1)}, bf16[512,128]{1,0:T(8,128)(2,1)S(1)}, u32[]{:S(2)}, u32[]{:S(2)}) collective-permute-start(bf16[512,128]{1,0:T(8,128)(2,1)S(1)} %get-tuple-element.60), channel_id=1, source_target_pairs={{0,127},{1,2},{2,1},{3,4},{4,3},{5,6},{6,5},{7,8},{8,7},{9,10},{10... | collective-permute-start | bytes 393224 | tf_op jit(solution)/shard_map/ppermute | solution.py:369
  53.8 0.0 collective-permute-done.2.got_e
  53.8 0.0 collective-permute-done.3.got_o
  53.8 1.4 %shard_map.69 = (bf16[1024,128]{1,0:T(8,128)(2,1)S(1)}, bf16[512,128]{1,0:T(8,128)(2,1)S(1)}, bf16[512,128]{1,0:T(8,128)(2,1)S(1)}) custom-call(f32[1024,128]{1,0:T(8,128)S(1)} %shard_map.67.base, bf16[1024,1024]{1,0:T(8,128)(2,1)S(1)} %get-tuple-element.49.edge, bf16[1024,1024]{1,0:T(8,128)(2,1)S(1)} %get-tuple-element.50.edge_t, ...), custom_call_target="tpu_custom_call" | custom-call | flops 536870912 | bytes 6000000 | tf_op jit(solution)/shard_map/pallas_call | solution.py:465
  55.1 0.1 collective-permute-start.6
  55.2 1.4 %collective-permute-start.7 = (bf16[512,128]{1,0:T(8,128)(2,1)S(1)}, bf16[512,128]{1,0:T(8,128)(2,1)S(1)}, u32[]{:S(2)}, u32[]{:S(2)}) collective-permute-start(bf16[512,128]{1,0:T(8,128)(2,1)S(1)} %get-tuple-element.58), channel_id=1, source_target_pairs={{0,127},{1,2},{2,1},{3,4},{4,3},{5,6},{6,5},{7,8},{8,7},{9,10},{10... | collective-permute-start | bytes 393224 | tf_op jit(solution)/shard_map/ppermute | solution.py:369
  56.6 0.7 shard_map.70.base
  57.3 0.9 collective-permute-done.9.got_o
  58.2 1.4 %shard_map.71 = (bf16[1024,128]{1,0:T(8,128)(2,1)S(1)}, bf16[512,128]{1,0:T(8,128)(2,1)S(1)}, bf16[512,128]{1,0:T(8,128)(2,1)S(1)}) custom-call(f32[1024,128]{1,0:T(8,128)S(1)} %shard_map.70.base, bf16[1024,1024]{1,0:T(8,128)(2,1)S(1)} %get-tuple-element.49.edge, bf16[1024,1024]{1,0:T(8,128)(2,1)S(1)} %get-tuple-element.50.edge_t, ...), custom_call_target="tpu_custom_call" | custom-call | flops 536870912 | bytes 6000000 | tf_op jit(solution)/shard_map/pallas_call | solution.py:461
  59.5 0.1 collective-permute-start.12
  59.6 6.0 %collective-permute-start.13 = (bf16[512,128]{1,0:T(8,128)(2,1)S(1)}, bf16[512,128]{1,0:T(8,128)(2,1)S(1)}, u32[]{:S(2)}, u32[]{:S(2)}) collective-permute-start(bf16[512,128]{1,0:T(8,128)(2,1)S(1)} %get-tuple-element.66), channel_id=1, source_target_pairs={{0,127},{1,2},{2,1},{3,4},{4,3},{5,6},{6,5},{7,8},{8,7},{9,10},{10... | collective-permute-start | bytes 393224 | tf_op jit(solution)/shard_map/ppermute | solution.py:369
  65.6 0.0 collective-permute-done.7.got_o
  65.6 1.4 %shard_map.72 = (bf16[1024,128]{1,0:T(8,128)(2,1)S(1)}, bf16[512,128]{1,0:T(8,128)(2,1)S(1)}, bf16[512,128]{1,0:T(8,128)(2,1)S(1)}) custom-call(f32[1024,128]{1,0:T(8,128)S(1)} %shard_map.70.base, bf16[1024,1024]{1,0:T(8,128)(2,1)S(1)} %get-tuple-element.49.edge, bf16[1024,1024]{1,0:T(8,128)(2,1)S(1)} %get-tuple-element.50.edge_t, ...), custom_call_target="tpu_custom_call" | custom-call | flops 536870912 | bytes 6000000 | tf_op jit(solution)/shard_map/pallas_call | solution.py:465
  67.0 0.1 collective-permute-start.10
  67.1 1.8 %collective-permute-start.11 = (bf16[512,128]{1,0:T(8,128)(2,1)S(1)}, bf16[512,128]{1,0:T(8,128)(2,1)S(1)}, u32[]{:S(2)}, u32[]{:S(2)}) collective-permute-start(bf16[512,128]{1,0:T(8,128)(2,1)S(1)} %get-tuple-element.64), channel_id=1, source_target_pairs={{0,127},{1,2},{2,1},{3,4},{4,3},{5,6},{6,5},{7,8},{8,7},{9,10},{10... | collective-permute-start | bytes 393224 | tf_op jit(solution)/shard_map/ppermute | solution.py:369
  68.9 0.7 shard_map.73.base
  69.6 0.0 collective-permute-done.13.got_o
  69.6 1.4 %shard_map.74 = (bf16[1024,128]{1,0:T(8,128)(2,1)S(1)}, bf16[512,128]{1,0:T(8,128)(2,1)S(1)}, bf16[512,128]{1,0:T(8,128)(2,1)S(1)}) custom-call(f32[1024,128]{1,0:T(8,128)S(1)} %shard_map.73.base, bf16[1024,1024]{1,0:T(8,128)(2,1)S(1)} %get-tuple-element.49.edge, bf16[1024,1024]{1,0:T(8,128)(2,1)S(1)} %get-tuple-element.50.edge_t, ...), custom_call_target="tpu_custom_call" | custom-call | flops 536870912 | bytes 6000000 | tf_op jit(solution)/shard_map/pallas_call | solution.py:461
  70.9 0.3 collective-permute-start.16
  71.3 6.8 %collective-permute-start.17 = (bf16[512,128]{1,0:T(8,128)(2,1)S(1)}, bf16[512,128]{1,0:T(8,128)(2,1)S(1)}, u32[]{:S(2)}, u32[]{:S(2)}) collective-permute-start(bf16[512,128]{1,0:T(8,128)(2,1)S(1)} %get-tuple-element.72), channel_id=1, source_target_pairs={{0,127},{1,2},{2,1},{3,4},{4,3},{5,6},{6,5},{7,8},{8,7},{9,10},{10... | collective-permute-start | bytes 393224 | tf_op jit(solution)/shard_map/ppermute | solution.py:369
  78.1 1.4 %shard_map.75 = (bf16[1024,128]{1,0:T(8,128)(2,1)S(1)}, bf16[512,128]{1,0:T(8,128)(2,1)S(1)}, bf16[512,128]{1,0:T(8,128)(2,1)S(1)}) custom-call(f32[1024,128]{1,0:T(8,128)S(1)} %shard_map.73.base, bf16[1024,1024]{1,0:T(8,128)(2,1)S(1)} %get-tuple-element.49.edge, bf16[1024,1024]{1,0:T(8,128)(2,1)S(1)} %get-tuple-element.50.edge_t, ...), custom_call_target="tpu_custom_call" | custom-call | flops 536870912 | bytes 6000000 | tf_op jit(solution)/shard_map/pallas_call | solution.py:465
  79.5 0.1 collective-permute-start.14
  79.5 1.4 %collective-permute-start.15 = (bf16[512,128]{1,0:T(8,128)(2,1)S(1)}, bf16[512,128]{1,0:T(8,128)(2,1)S(1)}, u32[]{:S(2)}, u32[]{:S(2)}) collective-permute-start(bf16[512,128]{1,0:T(8,128)(2,1)S(1)} %get-tuple-element.70), channel_id=1, source_target_pairs={{0,127},{1,2},{2,1},{3,4},{4,3},{5,6},{6,5},{7,8},{8,7},{9,10},{10... | collective-permute-start | bytes 393224 | tf_op jit(solution)/shard_map/ppermute | solution.py:369
  80.9 0.7 shard_map.76.base
  81.7 0.7 shard_map.77.y_in
  82.3 3.4 %collective-permute-done.14.got_e = bf16[512,128]{1,0:T(8,128)(2,1)S(1)} collective-permute-done((bf16[512,128]{1,0:T(8,128)(2,1)S(1)}, bf16[512,128]{1,0:T(8,128)(2,1)S(1)}, u32[]{:S(2)}, u32[]{:S(2)}) %collective-permute-start.14) | collective-permute-done | bytes 131104 | tf_op jit(solution)/shard_map/ppermute | solution.py:373
  85.8 4.4 %collective-permute-done.15.got_o = bf16[512,128]{1,0:T(8,128)(2,1)S(1)} collective-permute-done((bf16[512,128]{1,0:T(8,128)(2,1)S(1)}, bf16[512,128]{1,0:T(8,128)(2,1)S(1)}, u32[]{:S(2)}, u32[]{:S(2)}) %collective-permute-start.15) | collective-permute-done | bytes 131104 | tf_op jit(solution)/shard_map/ppermute | solution.py:369
  90.2 0.9 shard_map.78
  91.1 0.1 collective-permute-start.20
  91.2 0.1 collective-permute-start.19
  91.3 4.0 %collective-permute-start.18 = (f32[128,128]{1,0:T(8,128)S(1)}, f32[128,128]{1,0:T(8,128)S(1)}, u32[]{:S(2)}, u32[]{:S(2)}) collective-permute-start(f32[128,128]{1,0:T(8,128)S(1)} %get-tuple-element.73), channel_id=1, source_target_pairs={{0,1},{1,0},{2,3},{3,2},{4,5},{5,4},{6,7},{7,6},{8,9},{9,8},{10,11... | collective-permute-start | bytes 196616 | tf_op jit(solution)/shard_map/ppermute | solution.py:390
  95.3 2.1 %collective-permute-done.20 = f32[128,128]{1,0:T(8,128)S(1)} collective-permute-done((f32[128,128]{1,0:T(8,128)S(1)}, f32[128,128]{1,0:T(8,128)S(1)}, u32[]{:S(2)}, u32[]{:S(2)}) %collective-permute-start.20) | collective-permute-done | bytes 65568 | tf_op jit(solution)/shard_map/ppermute | solution.py:390
  97.4 0.9 collective-permute-done.18
  98.2 0.1 collective-permute-start.23
  98.3 0.1 collective-permute-start.22
  98.4 4.0 %collective-permute-start.21 = (f32[128,128]{1,0:T(8,128)S(1)}, f32[128,128]{1,0:T(8,128)S(1)}, u32[]{:S(2)}, u32[]{:S(2)}) collective-permute-start(f32[128,128]{1,0:T(8,128)S(1)} %add_add_fusion.2), channel_id=1, source_target_pairs={{0,4},{1,5},{2,6},{3,7},{4,0},{5,1},{6,2},{7,3},{8,12},{9,13},{10,... | collective-permute-start | bytes 196616 | tf_op jit(solution)/shard_map/ppermute | solution.py:390
  102.4 2.1 %collective-permute-done.23 = f32[128,128]{1,0:T(8,128)S(1)} collective-permute-done((f32[128,128]{1,0:T(8,128)S(1)}, f32[128,128]{1,0:T(8,128)S(1)}, u32[]{:S(2)}, u32[]{:S(2)}) %collective-permute-start.23) | collective-permute-done | bytes 65568 | tf_op jit(solution)/shard_map/ppermute | solution.py:390
  104.5 0.9 collective-permute-done.21
  105.4 0.1 collective-permute-start.24
  105.5 1.2 %collective-permute-done.24 = f32[128,128]{1,0:T(8,128)S(1)} collective-permute-done((f32[128,128]{1,0:T(8,128)S(1)}, f32[128,128]{1,0:T(8,128)S(1)}, u32[]{:S(2)}, u32[]{:S(2)}) %collective-permute-start.24) | collective-permute-done | bytes 65568 | tf_op jit(solution)/shard_map/ppermute | solution.py:390
  106.7 0.1 collective-permute-start.27
  106.8 0.1 collective-permute-start.26
  106.9 4.0 %collective-permute-start.25 = (f32[128,128]{1,0:T(8,128)S(1)}, f32[128,128]{1,0:T(8,128)S(1)}, u32[]{:S(2)}, u32[]{:S(2)}) collective-permute-start(f32[128,128]{1,0:T(8,128)S(1)} %add.36), channel_id=1, source_target_pairs={{0,32},{1,33},{2,34},{3,35},{4,36},{5,37},{6,38},{7,39},{8,40},{9,... | collective-permute-start | bytes 196616 | tf_op jit(solution)/shard_map/ppermute | solution.py:390
  110.9 2.7 %collective-permute-done.27 = f32[128,128]{1,0:T(8,128)S(1)} collective-permute-done((f32[128,128]{1,0:T(8,128)S(1)}, f32[128,128]{1,0:T(8,128)S(1)}, u32[]{:S(2)}, u32[]{:S(2)}) %collective-permute-start.27) | collective-permute-done | bytes 65568 | tf_op jit(solution)/shard_map/ppermute | solution.py:390
  113.6 0.6 collective-permute-done.25
  114.2 4.3 %shard_map.79 = f32[1024,128]{1,0:T(8,128)} custom-call(f32[128,128]{1,0:T(8,128)S(1)} %add_add_fusion.gram, bf16[1024,128]{1,0:T(8,128)(2,1)S(1)} %get-tuple-element.74.y), custom_call_target="tpu_custom_call" | custom-call | flops 536870912 | bytes 1000000 | tf_op jit(solution)/shard_map/pallas_call | solution.py:475
  (27 shorter events, 0.1 us)
Async XLA Ops:
  0.0 14.4 %copy-start.2 = (bf16[1024,128]{1,0:T(8,128)(2,1)S(1)}, bf16[1024,128]{1,0:T(8,128)(2,1)}, u32[]{:S(2)}) copy-start(bf16[1024,128]{1,0:T(8,128)(2,1)} %older.1) | copy-start | bytes 786436
  0.0 14.2 %copy-start.6 = (f32[1024]{0:T(1024)S(1)}, f32[1024]{0:T(1024)}, u32[]{:S(2)}) copy-start(f32[1024]{0:T(1024)} %param.10) | copy-start | bytes 12292
  5.4 19.3 %collective-permute-start = (bf16[3072,128]{1,0:T(8,128)(2,1)}, bf16[3072,128]{1,0:T(8,128)(2,1)S(1)}, u32[]{:S(2)}, u32[]{:S(2)}) collective-permute-start(bf16[3072,128]{1,0:T(8,128)(2,1)} %get-tuple-element.46.to_e), channel_id=1, source_target_pairs={{0,1},{1,0},{2,3},{3,2},{4,5},{5,4},{6,7},{7,6},{8,9},{9,8},{10,11... | collective-permute-start | bytes 2359304 | tf_op jit(solution)/shard_map/ppermute | solution.py:373
  7.1 24.6 %collective-permute-start.1 = (bf16[3072,128]{1,0:T(8,128)(2,1)}, bf16[3072,128]{1,0:T(8,128)(2,1)S(1)}, u32[]{:S(2)}, u32[]{:S(2)}) collective-permute-start(bf16[3072,128]{1,0:T(8,128)(2,1)} %get-tuple-element.47.to_o), channel_id=1, source_target_pairs={{0,127},{1,2},{2,1},{3,4},{4,3},{5,6},{6,5},{7,8},{8,7},{9,10},{10... | collective-permute-start | bytes 2359304 | tf_op jit(solution)/shard_map/ppermute | solution.py:369
  14.4 1.6 %copy-start = (bf16[1024,1024]{1,0:T(8,128)(2,1)S(1)}, bf16[1024,1024]{1,0:T(8,128)(2,1)}, u32[]{:S(2)}) copy-start(bf16[1024,1024]{1,0:T(8,128)(2,1)} %get-tuple-element.41.edge.edge_in) | copy-start | bytes 6291460
  16.0 1.6 %copy-start.3 = (bf16[1024,1024]{1,0:T(8,128)(2,1)S(1)}, bf16[1024,1024]{1,0:T(8,128)(2,1)}, u32[]{:S(2)}) copy-start(bf16[1024,1024]{1,0:T(8,128)(2,1)} %get-tuple-element.40.own) | copy-start | bytes 6291460
  17.6 14.1 %copy-start.1 = (bf16[1024,1024]{1,0:T(8,128)(2,1)S(1)}, bf16[1024,1024]{1,0:T(8,128)(2,1)}, u32[]{:S(2)}) copy-start(bf16[1024,1024]{1,0:T(8,128)(2,1)} %get-tuple-element.41.edge.edge_in) | copy-start | bytes 6291460
  17.6 14.1 %copy-start.4 = (bf16[3072,128]{1,0:T(8,128)(2,1)S(1)}, bf16[3072,128]{1,0:T(8,128)(2,1)}, u32[]{:S(2)}) copy-start(bf16[3072,128]{1,0:T(8,128)(2,1)} %get-tuple-element.46.to_e) | copy-start | bytes 2359300
  17.6 14.1 %copy-start.5 = (bf16[3072,128]{1,0:T(8,128)(2,1)S(1)}, bf16[3072,128]{1,0:T(8,128)(2,1)}, u32[]{:S(2)}) copy-start(bf16[3072,128]{1,0:T(8,128)(2,1)} %get-tuple-element.47.to_o) | copy-start | bytes 2359300
  34.6 9.2 %collective-permute-start.4 = (bf16[512,128]{1,0:T(8,128)(2,1)S(1)}, bf16[512,128]{1,0:T(8,128)(2,1)S(1)}, u32[]{:S(2)}, u32[]{:S(2)}) collective-permute-start(bf16[512,128]{1,0:T(8,128)(2,1)S(1)} %get-tuple-element.53), channel_id=1, source_target_pairs={{0,1},{1,0},{2,3},{3,2},{4,5},{5,4},{6,7},{7,6},{8,9},{9,8},{10,11... | collective-permute-start | bytes 393224 | tf_op jit(solution)/shard_map/ppermute | solution.py:373
  34.7 11.1 %collective-permute-start.5 = (bf16[512,128]{1,0:T(8,128)(2,1)S(1)}, bf16[512,128]{1,0:T(8,128)(2,1)S(1)}, u32[]{:S(2)}, u32[]{:S(2)}) collective-permute-start(bf16[512,128]{1,0:T(8,128)(2,1)S(1)} %get-tuple-element.54), channel_id=1, source_target_pairs={{0,127},{1,2},{2,1},{3,4},{4,3},{5,6},{6,5},{7,8},{8,7},{9,10},{10... | collective-permute-start | bytes 393224 | tf_op jit(solution)/shard_map/ppermute | solution.py:369
  41.7 12.0 %collective-permute-start.2 = (bf16[512,128]{1,0:T(8,128)(2,1)S(1)}, bf16[512,128]{1,0:T(8,128)(2,1)S(1)}, u32[]{:S(2)}, u32[]{:S(2)}) collective-permute-start(bf16[512,128]{1,0:T(8,128)(2,1)S(1)} %get-tuple-element.51), channel_id=1, source_target_pairs={{0,1},{1,0},{2,3},{3,2},{4,5},{5,4},{6,7},{7,6},{8,9},{9,8},{10,11... | collective-permute-start | bytes 393224 | tf_op jit(solution)/shard_map/ppermute | solution.py:373
  41.7 12.0 %collective-permute-start.3 = (bf16[512,128]{1,0:T(8,128)(2,1)S(1)}, bf16[512,128]{1,0:T(8,128)(2,1)S(1)}, u32[]{:S(2)}, u32[]{:S(2)}) collective-permute-start(bf16[512,128]{1,0:T(8,128)(2,1)S(1)} %get-tuple-element.52), channel_id=1, source_target_pairs={{0,127},{1,2},{2,1},{3,4},{4,3},{5,6},{6,5},{7,8},{8,7},{9,10},{10... | collective-permute-start | bytes 393224 | tf_op jit(solution)/shard_map/ppermute | solution.py:369
  47.1 10.1 %collective-permute-start.8 = (bf16[512,128]{1,0:T(8,128)(2,1)S(1)}, bf16[512,128]{1,0:T(8,128)(2,1)S(1)}, u32[]{:S(2)}, u32[]{:S(2)}) collective-permute-start(bf16[512,128]{1,0:T(8,128)(2,1)S(1)} %get-tuple-element.59), channel_id=1, source_target_pairs={{0,1},{1,0},{2,3},{3,2},{4,5},{5,4},{6,7},{7,6},{8,9},{9,8},{10,11... | collective-permute-start | bytes 393224 | tf_op jit(solution)/shard_map/ppermute | solution.py:373
  47.2 10.9 %collective-permute-start.9 = (bf16[512,128]{1,0:T(8,128)(2,1)S(1)}, bf16[512,128]{1,0:T(8,128)(2,1)S(1)}, u32[]{:S(2)}, u32[]{:S(2)}) collective-permute-start(bf16[512,128]{1,0:T(8,128)(2,1)S(1)} %get-tuple-element.60), channel_id=1, source_target_pairs={{0,127},{1,2},{2,1},{3,4},{4,3},{5,6},{6,5},{7,8},{8,7},{9,10},{10... | collective-permute-start | bytes 393224 | tf_op jit(solution)/shard_map/ppermute | solution.py:369
  55.1 10.5 %collective-permute-start.6 = (bf16[512,128]{1,0:T(8,128)(2,1)S(1)}, bf16[512,128]{1,0:T(8,128)(2,1)S(1)}, u32[]{:S(2)}, u32[]{:S(2)}) collective-permute-start(bf16[512,128]{1,0:T(8,128)(2,1)S(1)} %get-tuple-element.57), channel_id=1, source_target_pairs={{0,1},{1,0},{2,3},{3,2},{4,5},{5,4},{6,7},{7,6},{8,9},{9,8},{10,11... | collective-permute-start | bytes 393224 | tf_op jit(solution)/shard_map/ppermute | solution.py:373
  55.2 10.4 %collective-permute-start.7 = (bf16[512,128]{1,0:T(8,128)(2,1)S(1)}, bf16[512,128]{1,0:T(8,128)(2,1)S(1)}, u32[]{:S(2)}, u32[]{:S(2)}) collective-permute-start(bf16[512,128]{1,0:T(8,128)(2,1)S(1)} %get-tuple-element.58), channel_id=1, source_target_pairs={{0,127},{1,2},{2,1},{3,4},{4,3},{5,6},{6,5},{7,8},{8,7},{9,10},{10... | collective-permute-start | bytes 393224 | tf_op jit(solution)/shard_map/ppermute | solution.py:369
  59.5 10.1 %collective-permute-start.12 = (bf16[512,128]{1,0:T(8,128)(2,1)S(1)}, bf16[512,128]{1,0:T(8,128)(2,1)S(1)}, u32[]{:S(2)}, u32[]{:S(2)}) collective-permute-start(bf16[512,128]{1,0:T(8,128)(2,1)S(1)} %get-tuple-element.65), channel_id=1, source_target_pairs={{0,1},{1,0},{2,3},{3,2},{4,5},{5,4},{6,7},{7,6},{8,9},{9,8},{10,11... | collective-permute-start | bytes 393224 | tf_op jit(solution)/shard_map/ppermute | solution.py:373
  59.6 10.0 %collective-permute-start.13 = (bf16[512,128]{1,0:T(8,128)(2,1)S(1)}, bf16[512,128]{1,0:T(8,128)(2,1)S(1)}, u32[]{:S(2)}, u32[]{:S(2)}) collective-permute-start(bf16[512,128]{1,0:T(8,128)(2,1)S(1)} %get-tuple-element.66), channel_id=1, source_target_pairs={{0,127},{1,2},{2,1},{3,4},{4,3},{5,6},{6,5},{7,8},{8,7},{9,10},{10... | collective-permute-start | bytes 393224 | tf_op jit(solution)/shard_map/ppermute | solution.py:369
  67.0 11.1 %collective-permute-start.10 = (bf16[512,128]{1,0:T(8,128)(2,1)S(1)}, bf16[512,128]{1,0:T(8,128)(2,1)S(1)}, u32[]{:S(2)}, u32[]{:S(2)}) collective-permute-start(bf16[512,128]{1,0:T(8,128)(2,1)S(1)} %get-tuple-element.63), channel_id=1, source_target_pairs={{0,1},{1,0},{2,3},{3,2},{4,5},{5,4},{6,7},{7,6},{8,9},{9,8},{10,11... | collective-permute-start | bytes 393224 | tf_op jit(solution)/shard_map/ppermute | solution.py:373
  67.1 11.0 %collective-permute-start.11 = (bf16[512,128]{1,0:T(8,128)(2,1)S(1)}, bf16[512,128]{1,0:T(8,128)(2,1)S(1)}, u32[]{:S(2)}, u32[]{:S(2)}) collective-permute-start(bf16[512,128]{1,0:T(8,128)(2,1)S(1)} %get-tuple-element.64), channel_id=1, source_target_pairs={{0,127},{1,2},{2,1},{3,4},{4,3},{5,6},{6,5},{7,8},{8,7},{9,10},{10... | collective-permute-start | bytes 393224 | tf_op jit(solution)/shard_map/ppermute | solution.py:369
  70.9 10.7 %collective-permute-start.16 = (bf16[512,128]{1,0:T(8,128)(2,1)S(1)}, bf16[512,128]{1,0:T(8,128)(2,1)S(1)}, u32[]{:S(2)}, u32[]{:S(2)}) collective-permute-start(bf16[512,128]{1,0:T(8,128)(2,1)S(1)} %get-tuple-element.71), channel_id=1, source_target_pairs={{0,1},{1,0},{2,3},{3,2},{4,5},{5,4},{6,7},{7,6},{8,9},{9,8},{10,11... | collective-permute-start | bytes 393224 | tf_op jit(solution)/shard_map/ppermute | solution.py:373
  71.3 10.4 %collective-permute-start.17 = (bf16[512,128]{1,0:T(8,128)(2,1)S(1)}, bf16[512,128]{1,0:T(8,128)(2,1)S(1)}, u32[]{:S(2)}, u32[]{:S(2)}) collective-permute-start(bf16[512,128]{1,0:T(8,128)(2,1)S(1)} %get-tuple-element.72), channel_id=1, source_target_pairs={{0,127},{1,2},{2,1},{3,4},{4,3},{5,6},{6,5},{7,8},{8,7},{9,10},{10... | collective-permute-start | bytes 393224 | tf_op jit(solution)/shard_map/ppermute | solution.py:369
  79.5 6.3 %collective-permute-start.14 = (bf16[512,128]{1,0:T(8,128)(2,1)S(1)}, bf16[512,128]{1,0:T(8,128)(2,1)S(1)}, u32[]{:S(2)}, u32[]{:S(2)}) collective-permute-start(bf16[512,128]{1,0:T(8,128)(2,1)S(1)} %get-tuple-element.69), channel_id=1, source_target_pairs={{0,1},{1,0},{2,3},{3,2},{4,5},{5,4},{6,7},{7,6},{8,9},{9,8},{10,11... | collective-permute-start | bytes 393224 | tf_op jit(solution)/shard_map/ppermute | solution.py:373
  79.5 10.6 %collective-permute-start.15 = (bf16[512,128]{1,0:T(8,128)(2,1)S(1)}, bf16[512,128]{1,0:T(8,128)(2,1)S(1)}, u32[]{:S(2)}, u32[]{:S(2)}) collective-permute-start(bf16[512,128]{1,0:T(8,128)(2,1)S(1)} %get-tuple-element.70), channel_id=1, source_target_pairs={{0,127},{1,2},{2,1},{3,4},{4,3},{5,6},{6,5},{7,8},{8,7},{9,10},{10... | collective-permute-start | bytes 393224 | tf_op jit(solution)/shard_map/ppermute | solution.py:369
  91.1 6.3 %collective-permute-start.20 = (f32[128,128]{1,0:T(8,128)S(1)}, f32[128,128]{1,0:T(8,128)S(1)}, u32[]{:S(2)}, u32[]{:S(2)}) collective-permute-start(f32[128,128]{1,0:T(8,128)S(1)} %get-tuple-element.73), channel_id=1, source_target_pairs={{0,3},{1,2},{2,1},{3,0},{4,7},{5,6},{6,5},{7,4},{8,11},{9,10},{10,... | collective-permute-start | bytes 196616 | tf_op jit(solution)/shard_map/ppermute | solution.py:390
  91.2 6.2 %collective-permute-start.19 = (f32[128,128]{1,0:T(8,128)S(1)}, f32[128,128]{1,0:T(8,128)S(1)}, u32[]{:S(2)}, u32[]{:S(2)}) collective-permute-start(f32[128,128]{1,0:T(8,128)S(1)} %get-tuple-element.73), channel_id=1, source_target_pairs={{0,2},{1,3},{2,0},{3,1},{4,6},{5,7},{6,4},{7,5},{8,10},{9,11},{10,... | collective-permute-start | bytes 196616 | tf_op jit(solution)/shard_map/ppermute | solution.py:390
  91.3 6.9 %collective-permute-start.18 = (f32[128,128]{1,0:T(8,128)S(1)}, f32[128,128]{1,0:T(8,128)S(1)}, u32[]{:S(2)}, u32[]{:S(2)}) collective-permute-start(f32[128,128]{1,0:T(8,128)S(1)} %get-tuple-element.73), channel_id=1, source_target_pairs={{0,1},{1,0},{2,3},{3,2},{4,5},{5,4},{6,7},{7,6},{8,9},{9,8},{10,11... | collective-permute-start | bytes 196616 | tf_op jit(solution)/shard_map/ppermute | solution.py:390
  98.2 6.3 %collective-permute-start.23 = (f32[128,128]{1,0:T(8,128)S(1)}, f32[128,128]{1,0:T(8,128)S(1)}, u32[]{:S(2)}, u32[]{:S(2)}) collective-permute-start(f32[128,128]{1,0:T(8,128)S(1)} %add_add_fusion.2), channel_id=1, source_target_pairs={{0,12},{1,13},{2,14},{3,15},{4,8},{5,9},{6,10},{7,11},{8,4},{9,5},... | collective-permute-start | bytes 196616 | tf_op jit(solution)/shard_map/ppermute | solution.py:390
  98.3 6.2 %collective-permute-start.22 = (f32[128,128]{1,0:T(8,128)S(1)}, f32[128,128]{1,0:T(8,128)S(1)}, u32[]{:S(2)}, u32[]{:S(2)}) collective-permute-start(f32[128,128]{1,0:T(8,128)S(1)} %add_add_fusion.2), channel_id=1, source_target_pairs={{0,8},{1,9},{2,10},{3,11},{4,12},{5,13},{6,14},{7,15},{8,0},{9,1},... | collective-permute-start | bytes 196616 | tf_op jit(solution)/shard_map/ppermute | solution.py:390
  98.4 6.9 %collective-permute-start.21 = (f32[128,128]{1,0:T(8,128)S(1)}, f32[128,128]{1,0:T(8,128)S(1)}, u32[]{:S(2)}, u32[]{:S(2)}) collective-permute-start(f32[128,128]{1,0:T(8,128)S(1)} %add_add_fusion.2), channel_id=1, source_target_pairs={{0,4},{1,5},{2,6},{3,7},{4,0},{5,1},{6,2},{7,3},{8,12},{9,13},{10,... | collective-permute-start | bytes 196616 | tf_op jit(solution)/shard_map/ppermute | solution.py:390
  105.4 1.3 %collective-permute-start.24 = (f32[128,128]{1,0:T(8,128)S(1)}, f32[128,128]{1,0:T(8,128)S(1)}, u32[]{:S(2)}, u32[]{:S(2)}) collective-permute-start(f32[128,128]{1,0:T(8,128)S(1)} %add_add_fusion.1), channel_id=1, source_target_pairs={{0,16},{1,17},{2,18},{3,19},{4,20},{5,21},{6,22},{7,23},{8,24},{9,... | collective-permute-start | bytes 196616 | tf_op jit(solution)/shard_map/ppermute | solution.py:390
  106.7 6.8 %collective-permute-start.27 = (f32[128,128]{1,0:T(8,128)S(1)}, f32[128,128]{1,0:T(8,128)S(1)}, u32[]{:S(2)}, u32[]{:S(2)}) collective-permute-start(f32[128,128]{1,0:T(8,128)S(1)} %add.36), channel_id=1, source_target_pairs={{0,96},{1,97},{2,98},{3,99},{4,100},{5,101},{6,102},{7,103},{8,104... | collective-permute-start | bytes 196616 | tf_op jit(solution)/shard_map/ppermute | solution.py:390
  106.8 6.8 %collective-permute-start.26 = (f32[128,128]{1,0:T(8,128)S(1)}, f32[128,128]{1,0:T(8,128)S(1)}, u32[]{:S(2)}, u32[]{:S(2)}) collective-permute-start(f32[128,128]{1,0:T(8,128)S(1)} %add.36), channel_id=1, source_target_pairs={{0,64},{1,65},{2,66},{3,67},{4,68},{5,69},{6,70},{7,71},{8,72},{9,... | collective-permute-start | bytes 196616 | tf_op jit(solution)/shard_map/ppermute | solution.py:390
  106.9 7.2 %collective-permute-start.25 = (f32[128,128]{1,0:T(8,128)S(1)}, f32[128,128]{1,0:T(8,128)S(1)}, u32[]{:S(2)}, u32[]{:S(2)}) collective-permute-start(f32[128,128]{1,0:T(8,128)S(1)} %add.36), channel_id=1, source_target_pairs={{0,32},{1,33},{2,34},{3,35},{4,36},{5,37},{6,38},{7,39},{8,40},{9,... | collective-permute-start | bytes 196616 | tf_op jit(solution)/shard_map/ppermute | solution.py:390

commit v3 on v2

--- a/solution.py
+++ b/solution.py
@@ -232,7 +232,7 @@
     put(1, 1, 1, dot(edge_t[rows(3), :], spare[...]))
 
 
-def first_post_kernel(base, edge_in, edge_t_in, to_e, to_o, got_e, got_o, edge, edge_t, y, send_e, send_o, send_e2, send_o2, spare, sides):
+def first_post_kernel(base, edge_in, edge_t_in, to_e, to_o, got_e, got_o, edge, edge_t, y, send_e, send_o, spare, sides):
     edge[...] = edge_in[...]
     edge_t[...] = edge_t_in[...]
 
@@ -258,9 +258,13 @@
                         total += dot(read_block(source, i), got[pl.ds(halo + (p - start) * B, B), :])
             y[rows(a), :] = (0.5 * total).astype(BF16)
     by_parity(body)
-    for half, to_e, to_o in ((0, send_e, send_o), (1, send_e2, send_o2)):
-        pack(half, edge_t, y, sides, spare)
-        give(sides, to_e, to_o)
+    pack(0, edge_t, y, sides, spare)
+    give(sides, send_e, send_o)
+
+
+def second_pack_kernel(edge_t, y, send_e, send_o, spare, sides):
+    pack(1, edge_t, y, sides, spare)
+    give(sides, send_e, send_o)
 
 
 def local_kernel(sym, diag, y, older, base):
@@ -447,11 +451,11 @@
     sides = pltpu.VMEM((2, 2 * B, K), BF16)
     spare = [pltpu.VMEM((OWN, K), BF16), sides]
     edge, edge_t, y, *sends = call(
-        first_post_kernel, [square, square, tall, part, part, part, part], [VMEM] * 7, 3 * product, 9_000_000, spare, {1: 0, 2: 1}
+        first_post_kernel, [square, square, tall, part, part], [VMEM] * 7, 2 * product, 9_000_000, spare, {1: 0, 2: 1}
     )(base, edge, edge_t, to_e, to_o, got_e, got_o)
     older = y0
-    got = exchange(*sends[:2])
-    got2 = exchange(*sends[2:])
+    got = exchange(*sends)
+    got2 = exchange(*call(second_pack_kernel, [part, part], [VMEM] * 2, product, 3_000_000, spare)(edge_t, y))
     for step in range(1, DEG):
         base = call(local_kernel, [tall32], [VMEM] * 4, product, 3_500_000)(sym, diag, y, older)[0]
         older = y
@@ -469,7 +473,8 @@
         else:
             y = call(last_first_kernel, [tall], [VMEM] * 5, product, 4_000_000, [sides])(base, edge, *got, y)[0]
             y, gram = call(last_kernel, [tall, ((K, K), F32)], [VMEM] * 5, product, 4_000_000, [sides])(base, edge, *got2, y)
-    for stride, size in digits():
+    places = digits()
+    for stride, size in [places[i] for i in (2, 0, 1, 3)]:
         gram = group_sum(gram, stride, size)
     scale = float(np.sqrt(total * B))
     return call(

time: 119 us -> 118 us (level)
    ppermute x9, waiting for transfers between devices: 8.94 us -> 7.49 us  [swap_e(): lax.ppermute(value, AXES, [(i, i ^ 1) for i in range(lax.axis_size(AXES))])]
    pallas_call x1 -> x2, Pallas kernels: 2.93 us -> 3.25 us  [the longest x1 2.45 us: local(): call(first_post_kernel, [square, square, tall, part, part], [VMEM] * 7, 2...]
  transfers between devices with their start and end apart: 28 -> 28, of which waited for: 13 -> 15; matrix products, arithmetic and copies ran while one was open for 0% -> 0% of each run, Pallas kernels for 11% -> 12%
where the time goes in v3:
time: 118 us
  starting transfers between devices  54.8 us (46%)
  waiting for transfers between devices  32.4 us (27%)
  Pallas kernels  27.4 us (23%)
  local copies, waits for them, and re-layouts  3.41 us (3%)
    ppermute x9, starting transfers between devices, swap_o(): lax.ppermute(value, AXES, [(i, (i + 1 if i % 2 else i - 1) % count) for i...  39.8 us
    ppermute x9, waiting for transfers between devices, swap_o(): lax.ppermute(value, AXES, [(i, (i + 1 if i % 2 else i - 1) % count) for i...  14.5 us
    ppermute x10, starting transfers between devices, group_sum(): parts.append(lax.ppermute(value, AXES, pairs))  12.6 us
    ppermute x10, waiting for transfers between devices, group_sum(): parts.append(lax.ppermute(value, AXES, pairs))  10.4 us
    ppermute x9, waiting for transfers between devices, swap_e(): lax.ppermute(value, AXES, [(i, i ^ 1) for i in range(lax.axis_size(AXES))])  7.49 us
    pallas_call x1, Pallas kernels, local(): call(functools.partial(prep_kernel, total), [square, square, message, mes...  5.67 us
    pallas_call x1, Pallas kernels, local(): call(functools.partial(finish_kernel, scale), [tall32], [VMEM] * 2, 2 * p...  4.27 us
    pallas_call x3, Pallas kernels, local(): call(functools.partial(post_kernel, 1), outs, specs, 2 * product, 6000000...  4.06 us
  transfers between devices with their start and end apart: 28, of which 15 were waited for; matrix products, arithmetic and copies ran while one was open for 0% of the time, Pallas kernels for 12%

profile of v3, /device:TPU:0, one launch (start us, length us, event | category | flops | bytes accessed | tf_op | source)
XLA Modules:
  0.0 118.2 jit_solution(6658048418193465530)
XLA Ops:
  0.0 5.7 %shard_map.64 = (bf16[1024,1024]{1,0:T(8,128)(2,1)}, bf16[1024,1024]{1,0:T(8,128)(2,1)}, bf16[3072,128]{1,0:T(8,128)(2,1)}, bf16[3072,128]{1,0:T(8,128)(2,1)}) custom-call(f32[4,10]{1,0:T(4,128)} %scales_in.1, s32[4,10]{1,0:T(4,128)} %columns_in.1, s32[4]{0:T(128)} %live_in.1, bf16[4,10,256,256]{3,2,1,0:T(8,128)(2,1)} %blocks.1, bf16[1024,128]{1,0:T(8,128)(2,1)} %older.1), custom_call_target="tpu_custom_call" | custom-call | flops 268435456 | bytes 10000000 | tf_op jit(solution)/shard_map/pallas_call | solution.py:422
  5.7 1.6 %collective-permute-start = (bf16[3072,128]{1,0:T(8,128)(2,1)}, bf16[3072,128]{1,0:T(8,128)(2,1)S(1)}, u32[]{:S(2)}, u32[]{:S(2)}) collective-permute-start(bf16[3072,128]{1,0:T(8,128)(2,1)} %get-tuple-element.46.to_e), channel_id=1, source_target_pairs={{0,1},{1,0},{2,3},{3,2},{4,5},{5,4},{6,7},{7,6},{8,9},{9,8},{10,11... | collective-permute-start | bytes 2359304 | tf_op jit(solution)/shard_map/ppermute | solution.py:377
  7.3 7.0 %collective-permute-start.1 = (bf16[3072,128]{1,0:T(8,128)(2,1)}, bf16[3072,128]{1,0:T(8,128)(2,1)S(1)}, u32[]{:S(2)}, u32[]{:S(2)}) collective-permute-start(bf16[3072,128]{1,0:T(8,128)(2,1)} %get-tuple-element.47.to_o), channel_id=1, source_target_pairs={{0,127},{1,2},{2,1},{3,4},{4,3},{5,6},{6,5},{7,8},{8,7},{9,10},{10... | collective-permute-start | bytes 2359304 | tf_op jit(solution)/shard_map/ppermute | solution.py:373
  14.3 0.2 copy.9.onsite
  14.6 1.6 %copy-done = bf16[1024,1024]{1,0:T(8,128)(2,1)S(1)} copy-done((bf16[1024,1024]{1,0:T(8,128)(2,1)S(1)}, bf16[1024,1024]{1,0:T(8,128)(2,1)}, u32[]{:S(2)}) %copy-start) | copy-done | bytes 2097176
  16.2 1.6 %copy-done.3 = bf16[1024,1024]{1,0:T(8,128)(2,1)S(1)} copy-done((bf16[1024,1024]{1,0:T(8,128)(2,1)S(1)}, bf16[1024,1024]{1,0:T(8,128)(2,1)}, u32[]{:S(2)}) %copy-start.3) | copy-done | bytes 2097176
  17.8 1.6 %shard_map.65 = (f32[1024,1]{1,0:T(8,128)S(1)}, bf16[1024,1024]{1,0:T(8,128)(2,1)S(1)}, bf16[1024,1024]{1,0:T(8,128)(2,1)S(1)}, f32[1024,128]{1,0:T(8,128)S(1)}) custom-call(bf16[1024,1024]{1,0:T(8,128)(2,1)S(1)} %copy-done.3, bf16[1024,1024]{1,0:T(8,128)(2,1)S(1)} %copy-done, f32[1024,1]{1,0:T(8,128)S(1)} %copy.9.onsite, bf16[1024,128]{1,0:T(8,128)(2,1)S(1)} %copy-done.2), custom_call_target="tpu_custom_call" | custom-call | flops 268435456 | bytes 10000000 | tf_op jit(solution)/shard_map/pallas_call | solution.py:447
  19.4 5.7 %collective-permute-done.got_e = bf16[3072,128]{1,0:T(8,128)(2,1)S(1)} collective-permute-done((bf16[3072,128]{1,0:T(8,128)(2,1)}, bf16[3072,128]{1,0:T(8,128)(2,1)S(1)}, u32[]{:S(2)}, u32[]{:S(2)}) %collective-permute-start) | collective-permute-done | bytes 786464 | tf_op jit(solution)/shard_map/ppermute | solution.py:377
  25.1 6.9 %collective-permute-done.1.got_o = bf16[3072,128]{1,0:T(8,128)(2,1)S(1)} collective-permute-done((bf16[3072,128]{1,0:T(8,128)(2,1)}, bf16[3072,128]{1,0:T(8,128)(2,1)S(1)}, u32[]{:S(2)}, u32[]{:S(2)}) %collective-permute-start.1) | collective-permute-done | bytes 786464 | tf_op jit(solution)/shard_map/ppermute | solution.py:373
  32.0 2.5 %shard_map.66 = (bf16[1024,1024]{1,0:T(8,128)(2,1)S(1)}, bf16[1024,1024]{1,0:T(8,128)(2,1)S(1)}, bf16[1024,128]{1,0:T(8,128)(2,1)S(1)}, bf16[512,128]{1,0:T(8,128)(2,1)S(1)}, bf16[512,128]{1,0:T(8,128)(2,1)S(1)}) custom-call(f32[1024,128]{1,0:T(8,128)S(1)} %get-tuple-element.44.base, ...), custom_call_target="tpu_custom_call", output_to_operand_aliasing={{0}: (1, {}), {1}: (2, {})} | custom-call | flops 536870912 | bytes 9000000 | tf_op jit(solution)/shard_map/pallas_call | solution.py:453
  34.5 0.1 collective-permute-start.4
  34.6 6.9 %collective-permute-start.5 = (bf16[512,128]{1,0:T(8,128)(2,1)S(1)}, bf16[512,128]{1,0:T(8,128)(2,1)S(1)}, u32[]{:S(2)}, u32[]{:S(2)}) collective-permute-start(bf16[512,128]{1,0:T(8,128)(2,1)S(1)} %get-tuple-element.54), channel_id=1, source_target_pairs={{0,127},{1,2},{2,1},{3,4},{4,3},{5,6},{6,5},{7,8},{8,7},{9,10},{10... | collective-permute-start | bytes 393224 | tf_op jit(solution)/shard_map/ppermute | solution.py:373
  41.5 0.8 shard_map.68
  42.3 0.1 collective-permute-start.2
  42.4 1.4 %collective-permute-start.3 = (bf16[512,128]{1,0:T(8,128)(2,1)S(1)}, bf16[512,128]{1,0:T(8,128)(2,1)S(1)}, u32[]{:S(2)}, u32[]{:S(2)}) collective-permute-start(bf16[512,128]{1,0:T(8,128)(2,1)S(1)} %get-tuple-element.52), channel_id=1, source_target_pairs={{0,127},{1,2},{2,1},{3,4},{4,3},{5,6},{6,5},{7,8},{8,7},{9,10},{10... | collective-permute-start | bytes 393224 | tf_op jit(solution)/shard_map/ppermute | solution.py:373
  43.7 0.7 shard_map.67.base
  44.4 0.0 collective-permute-done.4.got_e
  44.5 0.9 collective-permute-done.5.got_o
  45.3 1.4 %shard_map.69 = (bf16[1024,128]{1,0:T(8,128)(2,1)S(1)}, bf16[512,128]{1,0:T(8,128)(2,1)S(1)}, bf16[512,128]{1,0:T(8,128)(2,1)S(1)}) custom-call(f32[1024,128]{1,0:T(8,128)S(1)} %shard_map.67.base, bf16[1024,1024]{1,0:T(8,128)(2,1)S(1)} %get-tuple-element.49.edge, bf16[1024,1024]{1,0:T(8,128)(2,1)S(1)} %get-tuple-element.50.edge_t, ...), custom_call_target="tpu_custom_call" | custom-call | flops 536870912 | bytes 6000000 | tf_op jit(solution)/shard_map/pallas_call | solution.py:465
  46.7 0.1 collective-permute-start.8
  46.8 6.9 %collective-permute-start.9 = (bf16[512,128]{1,0:T(8,128)(2,1)S(1)}, bf16[512,128]{1,0:T(8,128)(2,1)S(1)}, u32[]{:S(2)}, u32[]{:S(2)}) collective-permute-start(bf16[512,128]{1,0:T(8,128)(2,1)S(1)} %get-tuple-element.60), channel_id=1, source_target_pairs={{0,127},{1,2},{2,1},{3,4},{4,3},{5,6},{6,5},{7,8},{8,7},{9,10},{10... | collective-permute-start | bytes 393224 | tf_op jit(solution)/shard_map/ppermute | solution.py:373
  53.7 0.0 collective-permute-done.2.got_e
  53.7 1.4 %shard_map.70 = (bf16[1024,128]{1,0:T(8,128)(2,1)S(1)}, bf16[512,128]{1,0:T(8,128)(2,1)S(1)}, bf16[512,128]{1,0:T(8,128)(2,1)S(1)}) custom-call(f32[1024,128]{1,0:T(8,128)S(1)} %shard_map.67.base, bf16[1024,1024]{1,0:T(8,128)(2,1)S(1)} %get-tuple-element.49.edge, bf16[1024,1024]{1,0:T(8,128)(2,1)S(1)} %get-tuple-element.50.edge_t, ...), custom_call_target="tpu_custom_call" | custom-call | flops 536870912 | bytes 6000000 | tf_op jit(solution)/shard_map/pallas_call | solution.py:469
  55.1 0.1 collective-permute-start.6
  55.2 1.4 %collective-permute-start.7 = (bf16[512,128]{1,0:T(8,128)(2,1)S(1)}, bf16[512,128]{1,0:T(8,128)(2,1)S(1)}, u32[]{:S(2)}, u32[]{:S(2)}) collective-permute-start(bf16[512,128]{1,0:T(8,128)(2,1)S(1)} %get-tuple-element.58), channel_id=1, source_target_pairs={{0,127},{1,2},{2,1},{3,4},{4,3},{5,6},{6,5},{7,8},{8,7},{9,10},{10... | collective-permute-start | bytes 393224 | tf_op jit(solution)/shard_map/ppermute | solution.py:373
  56.6 0.7 shard_map.71.base
  57.3 1.0 collective-permute-done.9.got_o
  58.3 1.4 %shard_map.72 = (bf16[1024,128]{1,0:T(8,128)(2,1)S(1)}, bf16[512,128]{1,0:T(8,128)(2,1)S(1)}, bf16[512,128]{1,0:T(8,128)(2,1)S(1)}) custom-call(f32[1024,128]{1,0:T(8,128)S(1)} %shard_map.71.base, bf16[1024,1024]{1,0:T(8,128)(2,1)S(1)} %get-tuple-element.49.edge, bf16[1024,1024]{1,0:T(8,128)(2,1)S(1)} %get-tuple-element.50.edge_t, ...), custom_call_target="tpu_custom_call" | custom-call | flops 536870912 | bytes 6000000 | tf_op jit(solution)/shard_map/pallas_call | solution.py:465
  59.6 0.1 collective-permute-start.12
  59.7 6.1 %collective-permute-start.13 = (bf16[512,128]{1,0:T(8,128)(2,1)S(1)}, bf16[512,128]{1,0:T(8,128)(2,1)S(1)}, u32[]{:S(2)}, u32[]{:S(2)}) collective-permute-start(bf16[512,128]{1,0:T(8,128)(2,1)S(1)} %get-tuple-element.66), channel_id=1, source_target_pairs={{0,127},{1,2},{2,1},{3,4},{4,3},{5,6},{6,5},{7,8},{8,7},{9,10},{10... | collective-permute-start | bytes 393224 | tf_op jit(solution)/shard_map/ppermute | solution.py:373
  65.8 1.4 %shard_map.73 = (bf16[1024,128]{1,0:T(8,128)(2,1)S(1)}, bf16[512,128]{1,0:T(8,128)(2,1)S(1)}, bf16[512,128]{1,0:T(8,128)(2,1)S(1)}) custom-call(f32[1024,128]{1,0:T(8,128)S(1)} %shard_map.71.base, bf16[1024,1024]{1,0:T(8,128)(2,1)S(1)} %get-tuple-element.49.edge, bf16[1024,1024]{1,0:T(8,128)(2,1)S(1)} %get-tuple-element.50.edge_t, ...), custom_call_target="tpu_custom_call" | custom-call | flops 536870912 | bytes 6000000 | tf_op jit(solution)/shard_map/pallas_call | solution.py:469
  67.1 0.1 collective-permute-start.10
  67.2 1.9 %collective-permute-start.11 = (bf16[512,128]{1,0:T(8,128)(2,1)S(1)}, bf16[512,128]{1,0:T(8,128)(2,1)S(1)}, u32[]{:S(2)}, u32[]{:S(2)}) collective-permute-start(bf16[512,128]{1,0:T(8,128)(2,1)S(1)} %get-tuple-element.64), channel_id=1, source_target_pairs={{0,127},{1,2},{2,1},{3,4},{4,3},{5,6},{6,5},{7,8},{8,7},{9,10},{10... | collective-permute-start | bytes 393224 | tf_op jit(solution)/shard_map/ppermute | solution.py:373
  69.1 0.7 shard_map.74.base
  69.9 1.4 %shard_map.75 = (bf16[1024,128]{1,0:T(8,128)(2,1)S(1)}, bf16[512,128]{1,0:T(8,128)(2,1)S(1)}, bf16[512,128]{1,0:T(8,128)(2,1)S(1)}) custom-call(f32[1024,128]{1,0:T(8,128)S(1)} %shard_map.74.base, bf16[1024,1024]{1,0:T(8,128)(2,1)S(1)} %get-tuple-element.49.edge, bf16[1024,1024]{1,0:T(8,128)(2,1)S(1)} %get-tuple-element.50.edge_t, ...), custom_call_target="tpu_custom_call" | custom-call | flops 536870912 | bytes 6000000 | tf_op jit(solution)/shard_map/pallas_call | solution.py:465
  71.2 0.2 collective-permute-start.16
  71.4 6.4 %collective-permute-start.17 = (bf16[512,128]{1,0:T(8,128)(2,1)S(1)}, bf16[512,128]{1,0:T(8,128)(2,1)S(1)}, u32[]{:S(2)}, u32[]{:S(2)}) collective-permute-start(bf16[512,128]{1,0:T(8,128)(2,1)S(1)} %get-tuple-element.72), channel_id=1, source_target_pairs={{0,127},{1,2},{2,1},{3,4},{4,3},{5,6},{6,5},{7,8},{8,7},{9,10},{10... | collective-permute-start | bytes 393224 | tf_op jit(solution)/shard_map/ppermute | solution.py:373
  77.8 0.8 collective-permute-done.11.got_o
  78.6 1.4 %shard_map.76 = (bf16[1024,128]{1,0:T(8,128)(2,1)S(1)}, bf16[512,128]{1,0:T(8,128)(2,1)S(1)}, bf16[512,128]{1,0:T(8,128)(2,1)S(1)}) custom-call(f32[1024,128]{1,0:T(8,128)S(1)} %shard_map.74.base, bf16[1024,1024]{1,0:T(8,128)(2,1)S(1)} %get-tuple-element.49.edge, bf16[1024,1024]{1,0:T(8,128)(2,1)S(1)} %get-tuple-element.50.edge_t, ...), custom_call_target="tpu_custom_call" | custom-call | flops 536870912 | bytes 6000000 | tf_op jit(solution)/shard_map/pallas_call | solution.py:469
  80.0 0.1 collective-permute-start.14
  80.1 1.8 %collective-permute-start.15 = (bf16[512,128]{1,0:T(8,128)(2,1)S(1)}, bf16[512,128]{1,0:T(8,128)(2,1)S(1)}, u32[]{:S(2)}, u32[]{:S(2)}) collective-permute-start(bf16[512,128]{1,0:T(8,128)(2,1)S(1)} %get-tuple-element.70), channel_id=1, source_target_pairs={{0,127},{1,2},{2,1},{3,4},{4,3},{5,6},{6,5},{7,8},{8,7},{9,10},{10... | collective-permute-start | bytes 393224 | tf_op jit(solution)/shard_map/ppermute | solution.py:373
  81.9 0.7 shard_map.77.base
  82.6 0.7 shard_map.78.y_in
  83.3 1.7 %collective-permute-done.14.got_e = bf16[512,128]{1,0:T(8,128)(2,1)S(1)} collective-permute-done((bf16[512,128]{1,0:T(8,128)(2,1)S(1)}, bf16[512,128]{1,0:T(8,128)(2,1)S(1)}, u32[]{:S(2)}, u32[]{:S(2)}) %collective-permute-start.14) | collective-permute-done | bytes 131104 | tf_op jit(solution)/shard_map/ppermute | solution.py:377
  85.0 4.9 %collective-permute-done.15.got_o = bf16[512,128]{1,0:T(8,128)(2,1)S(1)} collective-permute-done((bf16[512,128]{1,0:T(8,128)(2,1)S(1)}, bf16[512,128]{1,0:T(8,128)(2,1)S(1)}, u32[]{:S(2)}, u32[]{:S(2)}) %collective-permute-start.15) | collective-permute-done | bytes 131104 | tf_op jit(solution)/shard_map/ppermute | solution.py:373
  90.0 0.9 shard_map.79
  90.9 0.1 collective-permute-start.18
  91.0 1.2 %collective-permute-done.18 = f32[128,128]{1,0:T(8,128)S(1)} collective-permute-done((f32[128,128]{1,0:T(8,128)S(1)}, f32[128,128]{1,0:T(8,128)S(1)}, u32[]{:S(2)}, u32[]{:S(2)}) %collective-permute-start.18) | collective-permute-done | bytes 65568 | tf_op jit(solution)/shard_map/ppermute | solution.py:394
  92.3 0.1 collective-permute-start.21
  92.3 0.1 collective-permute-start.20
  92.4 4.0 %collective-permute-start.19 = (f32[128,128]{1,0:T(8,128)S(1)}, f32[128,128]{1,0:T(8,128)S(1)}, u32[]{:S(2)}, u32[]{:S(2)}) collective-permute-start(f32[128,128]{1,0:T(8,128)S(1)} %add.30), channel_id=1, source_target_pairs={{0,1},{1,0},{2,3},{3,2},{4,5},{5,4},{6,7},{7,6},{8,9},{9,8},{10,11... | collective-permute-start | bytes 196616 | tf_op jit(solution)/shard_map/ppermute | solution.py:394
  96.4 2.7 %collective-permute-done.21 = f32[128,128]{1,0:T(8,128)S(1)} collective-permute-done((f32[128,128]{1,0:T(8,128)S(1)}, f32[128,128]{1,0:T(8,128)S(1)}, u32[]{:S(2)}, u32[]{:S(2)}) %collective-permute-start.21) | collective-permute-done | bytes 65568 | tf_op jit(solution)/shard_map/ppermute | solution.py:394
  99.1 0.6 collective-permute-done.19
  99.7 0.1 collective-permute-start.24
  99.8 0.1 collective-permute-start.23
  99.9 4.0 %collective-permute-start.22 = (f32[128,128]{1,0:T(8,128)S(1)}, f32[128,128]{1,0:T(8,128)S(1)}, u32[]{:S(2)}, u32[]{:S(2)}) collective-permute-start(f32[128,128]{1,0:T(8,128)S(1)} %add_add_fusion.2), channel_id=1, source_target_pairs={{0,4},{1,5},{2,6},{3,7},{4,0},{5,1},{6,2},{7,3},{8,12},{9,13},{10,... | collective-permute-start | bytes 196616 | tf_op jit(solution)/shard_map/ppermute | solution.py:394
  103.9 2.1 %collective-permute-done.24 = f32[128,128]{1,0:T(8,128)S(1)} collective-permute-done((f32[128,128]{1,0:T(8,128)S(1)}, f32[128,128]{1,0:T(8,128)S(1)}, u32[]{:S(2)}, u32[]{:S(2)}) %collective-permute-start.24) | collective-permute-done | bytes 65568 | tf_op jit(solution)/shard_map/ppermute | solution.py:394
  106.0 0.9 collective-permute-done.22
  106.8 0.7 collective-permute-start.27
  107.5 3.5 %collective-permute-start.25 = (f32[128,128]{1,0:T(8,128)S(1)}, f32[128,128]{1,0:T(8,128)S(1)}, u32[]{:S(2)}, u32[]{:S(2)}) collective-permute-start(f32[128,128]{1,0:T(8,128)S(1)} %add_add_fusion.1), channel_id=1, source_target_pairs={{0,32},{1,33},{2,34},{3,35},{4,36},{5,37},{6,38},{7,39},{8,40},{9,... | collective-permute-start | bytes 196616 | tf_op jit(solution)/shard_map/ppermute | solution.py:394
  111.0 1.4 %collective-permute-done.27 = f32[128,128]{1,0:T(8,128)S(1)} collective-permute-done((f32[128,128]{1,0:T(8,128)S(1)}, f32[128,128]{1,0:T(8,128)S(1)}, u32[]{:S(2)}, u32[]{:S(2)}) %collective-permute-start.27) | collective-permute-done | bytes 65568 | tf_op jit(solution)/shard_map/ppermute | solution.py:394
  112.4 0.9 collective-permute-done.26
  113.3 0.7 collective-permute-done.25
  114.0 4.3 %shard_map.80 = f32[1024,128]{1,0:T(8,128)} custom-call(f32[128,128]{1,0:T(8,128)S(1)} %add_add_fusion.gram, bf16[1024,128]{1,0:T(8,128)(2,1)S(1)} %get-tuple-element.74.y), custom_call_target="tpu_custom_call" | custom-call | flops 536870912 | bytes 1000000 | tf_op jit(solution)/shard_map/pallas_call | solution.py:480
  (28 shorter events, 0.1 us)
Async XLA Ops:
  0.0 14.6 %copy-start.2 = (bf16[1024,128]{1,0:T(8,128)(2,1)S(1)}, bf16[1024,128]{1,0:T(8,128)(2,1)}, u32[]{:S(2)}) copy-start(bf16[1024,128]{1,0:T(8,128)(2,1)} %older.1) | copy-start | bytes 786436
  0.0 14.3 %copy-start.6 = (f32[1024]{0:T(1024)S(1)}, f32[1024]{0:T(1024)}, u32[]{:S(2)}) copy-start(f32[1024]{0:T(1024)} %param.10) | copy-start | bytes 12292
  5.7 19.5 %collective-permute-start = (bf16[3072,128]{1,0:T(8,128)(2,1)}, bf16[3072,128]{1,0:T(8,128)(2,1)S(1)}, u32[]{:S(2)}, u32[]{:S(2)}) collective-permute-start(bf16[3072,128]{1,0:T(8,128)(2,1)} %get-tuple-element.46.to_e), channel_id=1, source_target_pairs={{0,1},{1,0},{2,3},{3,2},{4,5},{5,4},{6,7},{7,6},{8,9},{9,8},{10,11... | collective-permute-start | bytes 2359304 | tf_op jit(solution)/shard_map/ppermute | solution.py:377
  7.3 24.7 %collective-permute-start.1 = (bf16[3072,128]{1,0:T(8,128)(2,1)}, bf16[3072,128]{1,0:T(8,128)(2,1)S(1)}, u32[]{:S(2)}, u32[]{:S(2)}) collective-permute-start(bf16[3072,128]{1,0:T(8,128)(2,1)} %get-tuple-element.47.to_o), channel_id=1, source_target_pairs={{0,127},{1,2},{2,1},{3,4},{4,3},{5,6},{6,5},{7,8},{8,7},{9,10},{10... | collective-permute-start | bytes 2359304 | tf_op jit(solution)/shard_map/ppermute | solution.py:373
  14.6 1.6 %copy-start = (bf16[1024,1024]{1,0:T(8,128)(2,1)S(1)}, bf16[1024,1024]{1,0:T(8,128)(2,1)}, u32[]{:S(2)}) copy-start(bf16[1024,1024]{1,0:T(8,128)(2,1)} %get-tuple-element.41.edge.edge_in) | copy-start | bytes 6291460
  16.2 1.6 %copy-start.3 = (bf16[1024,1024]{1,0:T(8,128)(2,1)S(1)}, bf16[1024,1024]{1,0:T(8,128)(2,1)}, u32[]{:S(2)}) copy-start(bf16[1024,1024]{1,0:T(8,128)(2,1)} %get-tuple-element.40.own) | copy-start | bytes 6291460
  17.7 14.3 %copy-start.1 = (bf16[1024,1024]{1,0:T(8,128)(2,1)S(1)}, bf16[1024,1024]{1,0:T(8,128)(2,1)}, u32[]{:S(2)}) copy-start(bf16[1024,1024]{1,0:T(8,128)(2,1)} %get-tuple-element.41.edge.edge_in) | copy-start | bytes 6291460
  17.8 14.3 %copy-start.4 = (bf16[3072,128]{1,0:T(8,128)(2,1)S(1)}, bf16[3072,128]{1,0:T(8,128)(2,1)}, u32[]{:S(2)}) copy-start(bf16[3072,128]{1,0:T(8,128)(2,1)} %get-tuple-element.46.to_e) | copy-start | bytes 2359300
  17.8 14.3 %copy-start.5 = (bf16[3072,128]{1,0:T(8,128)(2,1)S(1)}, bf16[3072,128]{1,0:T(8,128)(2,1)}, u32[]{:S(2)}) copy-start(bf16[3072,128]{1,0:T(8,128)(2,1)} %get-tuple-element.47.to_o) | copy-start | bytes 2359300
  34.5 10.0 %collective-permute-start.4 = (bf16[512,128]{1,0:T(8,128)(2,1)S(1)}, bf16[512,128]{1,0:T(8,128)(2,1)S(1)}, u32[]{:S(2)}, u32[]{:S(2)}) collective-permute-start(bf16[512,128]{1,0:T(8,128)(2,1)S(1)} %get-tuple-element.53), channel_id=1, source_target_pairs={{0,1},{1,0},{2,3},{3,2},{4,5},{5,4},{6,7},{7,6},{8,9},{9,8},{10,11... | collective-permute-start | bytes 393224 | tf_op jit(solution)/shard_map/ppermute | solution.py:377
  34.6 10.8 %collective-permute-start.5 = (bf16[512,128]{1,0:T(8,128)(2,1)S(1)}, bf16[512,128]{1,0:T(8,128)(2,1)S(1)}, u32[]{:S(2)}, u32[]{:S(2)}) collective-permute-start(bf16[512,128]{1,0:T(8,128)(2,1)S(1)} %get-tuple-element.54), channel_id=1, source_target_pairs={{0,127},{1,2},{2,1},{3,4},{4,3},{5,6},{6,5},{7,8},{8,7},{9,10},{10... | collective-permute-start | bytes 393224 | tf_op jit(solution)/shard_map/ppermute | solution.py:373
  42.3 11.5 %collective-permute-start.2 = (bf16[512,128]{1,0:T(8,128)(2,1)S(1)}, bf16[512,128]{1,0:T(8,128)(2,1)S(1)}, u32[]{:S(2)}, u32[]{:S(2)}) collective-permute-start(bf16[512,128]{1,0:T(8,128)(2,1)S(1)} %get-tuple-element.51), channel_id=1, source_target_pairs={{0,1},{1,0},{2,3},{3,2},{4,5},{5,4},{6,7},{7,6},{8,9},{9,8},{10,11... | collective-permute-start | bytes 393224 | tf_op jit(solution)/shard_map/ppermute | solution.py:377
  42.4 11.4 %collective-permute-start.3 = (bf16[512,128]{1,0:T(8,128)(2,1)S(1)}, bf16[512,128]{1,0:T(8,128)(2,1)S(1)}, u32[]{:S(2)}, u32[]{:S(2)}) collective-permute-start(bf16[512,128]{1,0:T(8,128)(2,1)S(1)} %get-tuple-element.52), channel_id=1, source_target_pairs={{0,127},{1,2},{2,1},{3,4},{4,3},{5,6},{6,5},{7,8},{8,7},{9,10},{10... | collective-permute-start | bytes 393224 | tf_op jit(solution)/shard_map/ppermute | solution.py:373
  46.7 10.6 %collective-permute-start.8 = (bf16[512,128]{1,0:T(8,128)(2,1)S(1)}, bf16[512,128]{1,0:T(8,128)(2,1)S(1)}, u32[]{:S(2)}, u32[]{:S(2)}) collective-permute-start(bf16[512,128]{1,0:T(8,128)(2,1)S(1)} %get-tuple-element.59), channel_id=1, source_target_pairs={{0,1},{1,0},{2,3},{3,2},{4,5},{5,4},{6,7},{7,6},{8,9},{9,8},{10,11... | collective-permute-start | bytes 393224 | tf_op jit(solution)/shard_map/ppermute | solution.py:377
  46.8 11.5 %collective-permute-start.9 = (bf16[512,128]{1,0:T(8,128)(2,1)S(1)}, bf16[512,128]{1,0:T(8,128)(2,1)S(1)}, u32[]{:S(2)}, u32[]{:S(2)}) collective-permute-start(bf16[512,128]{1,0:T(8,128)(2,1)S(1)} %get-tuple-element.60), channel_id=1, source_target_pairs={{0,127},{1,2},{2,1},{3,4},{4,3},{5,6},{6,5},{7,8},{8,7},{9,10},{10... | collective-permute-start | bytes 393224 | tf_op jit(solution)/shard_map/ppermute | solution.py:373
  55.1 10.7 %collective-permute-start.6 = (bf16[512,128]{1,0:T(8,128)(2,1)S(1)}, bf16[512,128]{1,0:T(8,128)(2,1)S(1)}, u32[]{:S(2)}, u32[]{:S(2)}) collective-permute-start(bf16[512,128]{1,0:T(8,128)(2,1)S(1)} %get-tuple-element.57), channel_id=1, source_target_pairs={{0,1},{1,0},{2,3},{3,2},{4,5},{5,4},{6,7},{7,6},{8,9},{9,8},{10,11... | collective-permute-start | bytes 393224 | tf_op jit(solution)/shard_map/ppermute | solution.py:377
  55.2 10.6 %collective-permute-start.7 = (bf16[512,128]{1,0:T(8,128)(2,1)S(1)}, bf16[512,128]{1,0:T(8,128)(2,1)S(1)}, u32[]{:S(2)}, u32[]{:S(2)}) collective-permute-start(bf16[512,128]{1,0:T(8,128)(2,1)S(1)} %get-tuple-element.58), channel_id=1, source_target_pairs={{0,127},{1,2},{2,1},{3,4},{4,3},{5,6},{6,5},{7,8},{8,7},{9,10},{10... | collective-permute-start | bytes 393224 | tf_op jit(solution)/shard_map/ppermute | solution.py:373
  59.6 10.2 %collective-permute-start.12 = (bf16[512,128]{1,0:T(8,128)(2,1)S(1)}, bf16[512,128]{1,0:T(8,128)(2,1)S(1)}, u32[]{:S(2)}, u32[]{:S(2)}) collective-permute-start(bf16[512,128]{1,0:T(8,128)(2,1)S(1)} %get-tuple-element.65), channel_id=1, source_target_pairs={{0,1},{1,0},{2,3},{3,2},{4,5},{5,4},{6,7},{7,6},{8,9},{9,8},{10,11... | collective-permute-start | bytes 393224 | tf_op jit(solution)/shard_map/ppermute | solution.py:377
  59.7 10.1 %collective-permute-start.13 = (bf16[512,128]{1,0:T(8,128)(2,1)S(1)}, bf16[512,128]{1,0:T(8,128)(2,1)S(1)}, u32[]{:S(2)}, u32[]{:S(2)}) collective-permute-start(bf16[512,128]{1,0:T(8,128)(2,1)S(1)} %get-tuple-element.66), channel_id=1, source_target_pairs={{0,127},{1,2},{2,1},{3,4},{4,3},{5,6},{6,5},{7,8},{8,7},{9,10},{10... | collective-permute-start | bytes 393224 | tf_op jit(solution)/shard_map/ppermute | solution.py:373
  67.1 10.7 %collective-permute-start.10 = (bf16[512,128]{1,0:T(8,128)(2,1)S(1)}, bf16[512,128]{1,0:T(8,128)(2,1)S(1)}, u32[]{:S(2)}, u32[]{:S(2)}) collective-permute-start(bf16[512,128]{1,0:T(8,128)(2,1)S(1)} %get-tuple-element.63), channel_id=1, source_target_pairs={{0,1},{1,0},{2,3},{3,2},{4,5},{5,4},{6,7},{7,6},{8,9},{9,8},{10,11... | collective-permute-start | bytes 393224 | tf_op jit(solution)/shard_map/ppermute | solution.py:377
  67.2 11.4 %collective-permute-start.11 = (bf16[512,128]{1,0:T(8,128)(2,1)S(1)}, bf16[512,128]{1,0:T(8,128)(2,1)S(1)}, u32[]{:S(2)}, u32[]{:S(2)}) collective-permute-start(bf16[512,128]{1,0:T(8,128)(2,1)S(1)} %get-tuple-element.64), channel_id=1, source_target_pairs={{0,127},{1,2},{2,1},{3,4},{4,3},{5,6},{6,5},{7,8},{8,7},{9,10},{10... | collective-permute-start | bytes 393224 | tf_op jit(solution)/shard_map/ppermute | solution.py:373
  71.2 11.4 %collective-permute-start.16 = (bf16[512,128]{1,0:T(8,128)(2,1)S(1)}, bf16[512,128]{1,0:T(8,128)(2,1)S(1)}, u32[]{:S(2)}, u32[]{:S(2)}) collective-permute-start(bf16[512,128]{1,0:T(8,128)(2,1)S(1)} %get-tuple-element.71), channel_id=1, source_target_pairs={{0,1},{1,0},{2,3},{3,2},{4,5},{5,4},{6,7},{7,6},{8,9},{9,8},{10,11... | collective-permute-start | bytes 393224 | tf_op jit(solution)/shard_map/ppermute | solution.py:377
  71.4 11.2 %collective-permute-start.17 = (bf16[512,128]{1,0:T(8,128)(2,1)S(1)}, bf16[512,128]{1,0:T(8,128)(2,1)S(1)}, u32[]{:S(2)}, u32[]{:S(2)}) collective-permute-start(bf16[512,128]{1,0:T(8,128)(2,1)S(1)} %get-tuple-element.72), channel_id=1, source_target_pairs={{0,127},{1,2},{2,1},{3,4},{4,3},{5,6},{6,5},{7,8},{8,7},{9,10},{10... | collective-permute-start | bytes 393224 | tf_op jit(solution)/shard_map/ppermute | solution.py:373
  80.0 5.0 %collective-permute-start.14 = (bf16[512,128]{1,0:T(8,128)(2,1)S(1)}, bf16[512,128]{1,0:T(8,128)(2,1)S(1)}, u32[]{:S(2)}, u32[]{:S(2)}) collective-permute-start(bf16[512,128]{1,0:T(8,128)(2,1)S(1)} %get-tuple-element.69), channel_id=1, source_target_pairs={{0,1},{1,0},{2,3},{3,2},{4,5},{5,4},{6,7},{7,6},{8,9},{9,8},{10,11... | collective-permute-start | bytes 393224 | tf_op jit(solution)/shard_map/ppermute | solution.py:377
  80.1 9.9 %collective-permute-start.15 = (bf16[512,128]{1,0:T(8,128)(2,1)S(1)}, bf16[512,128]{1,0:T(8,128)(2,1)S(1)}, u32[]{:S(2)}, u32[]{:S(2)}) collective-permute-start(bf16[512,128]{1,0:T(8,128)(2,1)S(1)} %get-tuple-element.70), channel_id=1, source_target_pairs={{0,127},{1,2},{2,1},{3,4},{4,3},{5,6},{6,5},{7,8},{8,7},{9,10},{10... | collective-permute-start | bytes 393224 | tf_op jit(solution)/shard_map/ppermute | solution.py:373
  90.9 1.3 %collective-permute-start.18 = (f32[128,128]{1,0:T(8,128)S(1)}, f32[128,128]{1,0:T(8,128)S(1)}, u32[]{:S(2)}, u32[]{:S(2)}) collective-permute-start(f32[128,128]{1,0:T(8,128)S(1)} %get-tuple-element.73), channel_id=1, source_target_pairs={{0,16},{1,17},{2,18},{3,19},{4,20},{5,21},{6,22},{7,23},{8,24},{9,... | collective-permute-start | bytes 196616 | tf_op jit(solution)/shard_map/ppermute | solution.py:394
  92.3 6.8 %collective-permute-start.21 = (f32[128,128]{1,0:T(8,128)S(1)}, f32[128,128]{1,0:T(8,128)S(1)}, u32[]{:S(2)}, u32[]{:S(2)}) collective-permute-start(f32[128,128]{1,0:T(8,128)S(1)} %add.30), channel_id=1, source_target_pairs={{0,3},{1,2},{2,1},{3,0},{4,7},{5,6},{6,5},{7,4},{8,11},{9,10},{10,... | collective-permute-start | bytes 196616 | tf_op jit(solution)/shard_map/ppermute | solution.py:394
  92.3 6.8 %collective-permute-start.20 = (f32[128,128]{1,0:T(8,128)S(1)}, f32[128,128]{1,0:T(8,128)S(1)}, u32[]{:S(2)}, u32[]{:S(2)}) collective-permute-start(f32[128,128]{1,0:T(8,128)S(1)} %add.30), channel_id=1, source_target_pairs={{0,2},{1,3},{2,0},{3,1},{4,6},{5,7},{6,4},{7,5},{8,10},{9,11},{10,... | collective-permute-start | bytes 196616 | tf_op jit(solution)/shard_map/ppermute | solution.py:394
  92.4 7.2 %collective-permute-start.19 = (f32[128,128]{1,0:T(8,128)S(1)}, f32[128,128]{1,0:T(8,128)S(1)}, u32[]{:S(2)}, u32[]{:S(2)}) collective-permute-start(f32[128,128]{1,0:T(8,128)S(1)} %add.30), channel_id=1, source_target_pairs={{0,1},{1,0},{2,3},{3,2},{4,5},{5,4},{6,7},{7,6},{8,9},{9,8},{10,11... | collective-permute-start | bytes 196616 | tf_op jit(solution)/shard_map/ppermute | solution.py:394
  99.7 6.3 %collective-permute-start.24 = (f32[128,128]{1,0:T(8,128)S(1)}, f32[128,128]{1,0:T(8,128)S(1)}, u32[]{:S(2)}, u32[]{:S(2)}) collective-permute-start(f32[128,128]{1,0:T(8,128)S(1)} %add_add_fusion.2), channel_id=1, source_target_pairs={{0,12},{1,13},{2,14},{3,15},{4,8},{5,9},{6,10},{7,11},{8,4},{9,5},... | collective-permute-start | bytes 196616 | tf_op jit(solution)/shard_map/ppermute | solution.py:394
  99.8 6.2 %collective-permute-start.23 = (f32[128,128]{1,0:T(8,128)S(1)}, f32[128,128]{1,0:T(8,128)S(1)}, u32[]{:S(2)}, u32[]{:S(2)}) collective-permute-start(f32[128,128]{1,0:T(8,128)S(1)} %add_add_fusion.2), channel_id=1, source_target_pairs={{0,8},{1,9},{2,10},{3,11},{4,12},{5,13},{6,14},{7,15},{8,0},{9,1},... | collective-permute-start | bytes 196616 | tf_op jit(solution)/shard_map/ppermute | solution.py:394
  99.9 6.9 %collective-permute-start.22 = (f32[128,128]{1,0:T(8,128)S(1)}, f32[128,128]{1,0:T(8,128)S(1)}, u32[]{:S(2)}, u32[]{:S(2)}) collective-permute-start(f32[128,128]{1,0:T(8,128)S(1)} %add_add_fusion.2), channel_id=1, source_target_pairs={{0,4},{1,5},{2,6},{3,7},{4,0},{5,1},{6,2},{7,3},{8,12},{9,13},{10,... | collective-permute-start | bytes 196616 | tf_op jit(solution)/shard_map/ppermute | solution.py:394
  106.8 5.6 %collective-permute-start.27 = (f32[128,128]{1,0:T(8,128)S(1)}, f32[128,128]{1,0:T(8,128)S(1)}, u32[]{:S(2)}, u32[]{:S(2)}) collective-permute-start(f32[128,128]{1,0:T(8,128)S(1)} %add_add_fusion.1), channel_id=1, source_target_pairs={{0,96},{1,97},{2,98},{3,99},{4,100},{5,101},{6,102},{7,103},{8,104... | collective-permute-start | bytes 196616 | tf_op jit(solution)/shard_map/ppermute | solution.py:394
  107.5 5.8 %collective-permute-start.26 = (f32[128,128]{1,0:T(8,128)S(1)}, f32[128,128]{1,0:T(8,128)S(1)}, u32[]{:S(2)}, u32[]{:S(2)}) collective-permute-start(f32[128,128]{1,0:T(8,128)S(1)} %add_add_fusion.1), channel_id=1, source_target_pairs={{0,64},{1,65},{2,66},{3,67},{4,68},{5,69},{6,70},{7,71},{8,72},{9,... | collective-permute-start | bytes 196616 | tf_op jit(solution)/shard_map/ppermute | solution.py:394
  107.5 6.4 %collective-permute-start.25 = (f32[128,128]{1,0:T(8,128)S(1)}, f32[128,128]{1,0:T(8,128)S(1)}, u32[]{:S(2)}, u32[]{:S(2)}) collective-permute-start(f32[128,128]{1,0:T(8,128)S(1)} %add_add_fusion.1), channel_id=1, source_target_pairs={{0,32},{1,33},{2,34},{3,35},{4,36},{5,37},{6,38},{7,39},{8,40},{9,... | collective-permute-start | bytes 196616 | tf_op jit(solution)/shard_map/ppermute | solution.py:394
